TPU v7x, 128 devices: a whole 4x4x4 slice. The times are simulated.
128 devices in a mesh: row: 16 (over z_lo, x, core), col: 8 (over z_hi, y).
Axes of the slice: x: 4, y: 4, z: 4 (z_hi: 2, z_lo: 2; z = z_hi * 2 + z_lo), core: 2. Of those that a mesh axis runs over, the one named last changes fastest.
Arguments:
- queries: bfloat16 [256, 512, 1024], P('row', 'col'), may hold values from -6.5 to 6.5
- keys: bfloat16 [256, 512, 1024], P('row', 'col'), may hold values from -6.5 to 6.5
- values: bfloat16 [256, 512, 1024], P('row', 'col'), may hold values from -6 to 6
- grad_output: bfloat16 [256, 512, 1024], P('row', 'col'), may hold values from -6 to 6
Outputs:
- attended: bfloat16 [256, 512, 1024], P('row', 'col')
- query_grad: bfloat16 [256, 512, 1024], P('row', 'col')
- key_grad: bfloat16 [256, 512, 1024], P('row', 'col')
- value_grad: bfloat16 [256, 512, 1024], P('row', 'col')
All inputs are finite; a program needn't handle non-finite values.
Results may differ from a plain program's by a relative error of at most 0.0059.
Values may be sent and summed in bfloat16 or wider, within the bound.
A program may use at most 192 MiB of HBM per device.

v0:
```python
import jax
import jax.numpy as jnp
from jax import lax
from jax.sharding import PartitionSpec as P

HEAD_DIM = 64


def causal_mask(count_q, count_k):
    query_pos = lax.broadcasted_iota(jnp.int32, (count_q, count_k), 0)
    key_pos = lax.broadcasted_iota(jnp.int32, (count_q, count_k), 1)
    return key_pos <= query_pos


def attend(query, key, value, grad_out, allowed):
    score_scale = query.shape[-1] ** (-0.5)
    scores = (
        jnp.einsum("bqhd,bkhd->bhqk", query, key, preferred_element_type=jnp.float32) * score_scale
    )
    scores = jnp.where(allowed, scores, -1e30)
    row_max = jnp.max(scores, axis=-1, keepdims=True)
    weights = jnp.exp(scores - row_max)
    probs = weights / jnp.sum(weights, axis=-1, keepdims=True)
    probs_low = probs.astype(jnp.bfloat16)
    attended = jnp.einsum("bhqk,bkhd->bqhd", probs_low, value, preferred_element_type=jnp.float32)
    dprobs = jnp.einsum("bqhd,bkhd->bhqk", grad_out, value, preferred_element_type=jnp.float32)
    row_delta = jnp.sum(probs * dprobs, axis=-1, keepdims=True)
    dscores = (probs * (dprobs - row_delta)).astype(jnp.bfloat16)
    dquery = (
        jnp.einsum("bhqk,bkhd->bqhd", dscores, key, preferred_element_type=jnp.float32)
        * score_scale
    )
    key_grad = (
        jnp.einsum("bhqk,bqhd->bkhd", dscores, query, preferred_element_type=jnp.float32)
        * score_scale
    )
    value_grad = jnp.einsum(
        "bhqk,bqhd->bkhd", probs_low, grad_out, preferred_element_type=jnp.float32
    )
    return (attended, dquery, key_grad, value_grad)


def split_heads(array):
    return array.reshape(array.shape[:-1] + (array.shape[-1] // HEAD_DIM, HEAD_DIM))


def merge_heads(array):
    return array.reshape(array.shape[:-2] + (array.shape[-2] * array.shape[-1],))


def row_work(pieces):
    query_part, key_part, value_part, grad_part = [split_heads(piece) for piece in pieces]
    length = query_part.shape[1]
    results = attend(query_part, key_part, value_part, grad_part, causal_mask(length, length))
    return tuple((merge_heads(result).astype(jnp.bfloat16) for result in results))


def column_work(pieces):
    query_part, key_part, value_part, grad_part = [
        jnp.swapaxes(split_heads(piece[:, 0]), 0, 1) for piece in pieces
    ]
    length = query_part.shape[1]
    results = attend(query_part, key_part, value_part, grad_part, causal_mask(length, length))
    return tuple(
        (
            jnp.swapaxes(merge_heads(result).astype(jnp.bfloat16), 0, 1)[:, None]
            for result in results
        )
    )


def row_heads(queries, keys, values, grad_output, half_width):
    inputs = (
        queries[:, :, :half_width],
        keys[:, :, :half_width],
        values[:, :, :half_width],
        grad_output[:, :, :half_width],
    )
    done_out, done_query, done_key, done_value = row_work(
        (
            lax.all_to_all(inputs[0], "col", split_axis=2, concat_axis=1, tiled=True),
            lax.all_to_all(inputs[1], "col", split_axis=2, concat_axis=1, tiled=True),
            lax.all_to_all(inputs[2], "col", split_axis=2, concat_axis=1, tiled=True),
            lax.all_to_all(inputs[3], "col", split_axis=2, concat_axis=1, tiled=True),
        )
    )
    return (
        lax.all_to_all(done_out, "col", split_axis=1, concat_axis=2, tiled=True),
        lax.all_to_all(done_query, "col", split_axis=1, concat_axis=2, tiled=True),
        lax.all_to_all(done_key, "col", split_axis=1, concat_axis=2, tiled=True),
        lax.all_to_all(done_value, "col", split_axis=1, concat_axis=2, tiled=True),
    )


def column_heads(queries, keys, values, grad_output, half_width):
    groups = lax.axis_size("row")
    local_rows = queries.shape[0]
    per_group = queries.shape[1] // groups
    width = queries.shape[2] - half_width

    def grouped(array):
        return array[:, :, half_width:].reshape(local_rows, groups, per_group, width)

    inputs = (grouped(queries), grouped(keys), grouped(values), grouped(grad_output))
    moved_out, moved_query, moved_key, moved_value = column_work(
        (
            lax.all_to_all(inputs[0], "row", split_axis=1, concat_axis=0, tiled=True),
            lax.all_to_all(inputs[1], "row", split_axis=1, concat_axis=0, tiled=True),
            lax.all_to_all(inputs[2], "row", split_axis=1, concat_axis=0, tiled=True),
            lax.all_to_all(inputs[3], "row", split_axis=1, concat_axis=0, tiled=True),
        )
    )
    back = (
        lax.all_to_all(moved_out, "row", split_axis=0, concat_axis=1, tiled=True),
        lax.all_to_all(moved_query, "row", split_axis=0, concat_axis=1, tiled=True),
        lax.all_to_all(moved_key, "row", split_axis=0, concat_axis=1, tiled=True),
        lax.all_to_all(moved_value, "row", split_axis=0, concat_axis=1, tiled=True),
    )
    return tuple((item.reshape(local_rows, groups * per_group, width) for item in back))


def on_device(queries, keys, values, grad_output):
    half_width = queries.shape[2] // 2
    row_parts = row_heads(queries, keys, values, grad_output, half_width)
    column_parts = column_heads(queries, keys, values, grad_output, half_width)
    joined = [
        jnp.concatenate([first, second], axis=2) for first, second in zip(row_parts, column_parts)
    ]
    return (joined[0], joined[1], joined[2], joined[3])


def solution(mesh):
    in_specs = (
        P("row", "col", None),
        P("row", "col", None),
        P("row", "col", None),
        P("row", "col", None),
    )
    out_specs = (
        P("row", "col", None),
        P("row", "col", None),
        P("row", "col", None),
        P("row", "col", None),
    )
    return jax.shard_map(
        on_device, mesh=mesh, in_specs=in_specs, out_specs=out_specs, check_vma=False
    )
```

profile of v0, /device:TPU:1, one launch (start us, length us, event | category | flops | bytes accessed | tf_op | source)
XLA Modules:
  0.0 477.7 jit_solution(14112933171454757423)
XLA Ops:
  8.0 8.3 %all-to-all-start = ((bf16[8,2,32768]{2,1,0:T(2,128)(2,1)}), bf16[8,2,32768]{2,1,0:T(2,128)(2,1)S(1)}, u32[]{:S(2)}, u32[]{:S(2)}) async-start(bf16[8,2,32768]{2,1,0:T(2,128)(2,1)} %reshape.148), calls=%async_computation | async-start | bytes 2097152 | tf_op jit(solution)/shard_map/all_to_all | solution.py:81
  16.4 3.1 fusion.47
  25.1 8.6 %all-to-all-done = bf16[8,2,32768]{2,1,0:T(2,128)(2,1)S(1)} async-done(((bf16[8,2,32768]{2,1,0:T(2,128)(2,1)}), bf16[8,2,32768]{2,1,0:T(2,128)(2,1)S(1)}, u32[]{:S(2)}, u32[]{:S(2)}) %all-to-all-start) | async-done | bytes 1048608 | tf_op jit(solution)/shard_map/all_to_all | solution.py:81
  33.7 4.3 all-to-all-start.1
  37.9 3.1 fusion.49
  46.7 8.6 %all-to-all-done.1 = bf16[8,2,32768]{2,1,0:T(2,128)(2,1)} async-done(((bf16[8,2,32768]{2,1,0:T(2,128)(2,1)}), bf16[8,2,32768]{2,1,0:T(2,128)(2,1)}, u32[]{:S(2)}, u32[]{:S(2)}) %all-to-all-start.1) | async-done | bytes 1048608 | tf_op jit(solution)/shard_map/all_to_all | solution.py:82
  55.3 4.2 all-to-all-start.2
  59.5 3.1 fusion.46
  68.3 8.6 %all-to-all-done.2 = bf16[8,2,32768]{2,1,0:T(2,128)(2,1)} async-done(((bf16[8,2,32768]{2,1,0:T(2,128)(2,1)}), bf16[8,2,32768]{2,1,0:T(2,128)(2,1)}, u32[]{:S(2)}, u32[]{:S(2)}) %all-to-all-start.2) | async-done | bytes 1048608 | tf_op jit(solution)/shard_map/all_to_all | solution.py:83
  76.9 4.4 all-to-all-start.8
  93.1 4.1 reshape.134
  97.1 3.1 reshape.151
  102.9 3.2 reshape.135
  106.1 3.1 reshape.147
  111.9 4.0 reshape.136
  115.9 6.0 %all-to-all-start.4 = ((bf16[16,16,4,512]{3,0,2,1:T(8,128)(2,1)}), bf16[16,16,4,512]{3,0,2,1:T(8,128)(2,1)}, u32[]{:S(2)}, u32[]{:S(2)}) async-start(bf16[16,16,4,512]{3,0,2,1:T(8,128)(2,1)} %bitcast.216), calls=%async_computation.4 | async-start | bytes 2097152 | tf_op jit(solution)/shard_map/all_to_all | solution.py:107
  121.9 3.1 reshape.155
  127.7 3.2 reshape.141
  130.9 11.0 %fusion.51 = (f32[16,512]{1,0:T(8,128)S(1)}, f32[16,512,512]{1,2,0:T(8,128)}) fusion(pred[512,512]{0,1:T(8,128)(4,1)S(1)} %iota_compare_fusion, bf16[16,512,64]{1,2,0:T(8,128)(2,1)} %reshape.134, bf16[16,512,64]{1,2,0:T(8,128)(2,1)S(1)} %reshape.135), kind=kOutput, calls=%fused_computation.70 | convolution fusion | flops 553648640 | bytes 19169280 | tf_op jit(solution)/shard_map/sub | solution.py:22
  141.9 10.7 %multiply_reduce_fusion = (f32[16,512]{1,0:T(8,128)S(1)}, f32[16,512,512]{1,2,0:T(8,128)}) fusion(f32[16,512,512]{1,2,0:T(8,128)} %get-tuple-element.23, f32[16,512]{1,0:T(8,128)S(1)} %get-tuple-element.22, bf16[16,512,64]{1,2,0:T(8,128)(2,1)S(1)} %reshape.141, bf16[16,512,64]{1,2,0:T(8,128)(2,1)S(1)} %copy-done.16), kind=kOutput, calls=%fused_computation.3 | convolution fusion | flops 549445632 | bytes 35717120 | tf_op jit(solution)/shard_map/bqhd,bkhd->bhqk/dot_general | solution.py:26
  152.6 5.7 %all-to-all-start.5 = ((bf16[16,16,4,512]{3,0,2,1:T(8,128)(2,1)}), bf16[16,16,4,512]{3,0,2,1:T(8,128)(2,1)S(1)}, u32[]{:S(2)}, u32[]{:S(2)}) async-start(bf16[16,16,4,512]{3,0,2,1:T(8,128)(2,1)} %bitcast.12), calls=%async_computation.5 | async-start | bytes 2097152 | tf_op jit(solution)/shard_map/all_to_all | solution.py:108
  158.3 15.2 %multiply_convert_fusion = bf16[16,512,512]{1,2,0:T(8,128)(2,1)} fusion(f32[16,512,512]{1,2,0:T(8,128)} %get-tuple-element.27, f32[16,512]{1,0:T(8,128)S(1)} %get-tuple-element.26, f32[16,512,512]{1,2,0:T(8,128)} %get-tuple-element.23, f32[16,512]{1,0:T(8,128)S(1)} %get-tuple-element.22), kind=kLoop, calls=%fused_computation.2 | loop fusion | flops 16777216 | bytes 42008576 | tf_op jit(solution)/shard_map/convert_element_type | solution.py:28
  175.1 5.0 %all-to-all-start.6 = ((bf16[16,16,4,512]{3,0,2,1:T(8,128)(2,1)}), bf16[16,16,4,512]{3,0,2,1:T(8,128)(2,1)S(1)}, u32[]{:S(2)}, u32[]{:S(2)}) async-start(bf16[16,16,4,512]{3,0,2,1:T(8,128)(2,1)} %bitcast.16), calls=%async_computation.6 | async-start | bytes 2097152 | tf_op jit(solution)/shard_map/all_to_all | solution.py:109
  180.2 9.6 %fusion.29 = bf16[16,512,64]{1,2,0:T(8,128)(2,1)} fusion(bf16[16,512,64]{1,2,0:T(8,128)(2,1)} %copy-done.17, f32[16,512,512]{1,2,0:T(8,128)} %get-tuple-element.23, f32[16,512]{1,0:T(8,128)S(1)} %get-tuple-element.22), kind=kOutput, calls=%fused_computation.48 | convolution fusion | flops 545783808 | bytes 18907136 | tf_op jit(solution)/shard_map/bhqk,bqhd->bkhd/dot_general | solution.py:37
  189.8 6.2 %all-to-all-done.6 = bf16[16,16,4,512]{3,0,2,1:T(8,128)(2,1)S(1)} async-done(((bf16[16,16,4,512]{3,0,2,1:T(8,128)(2,1)}), bf16[16,16,4,512]{3,0,2,1:T(8,128)(2,1)S(1)}, u32[]{:S(2)}, u32[]{:S(2)}) %all-to-all-start.6) | async-done | bytes 1048608 | tf_op jit(solution)/shard_map/all_to_all | solution.py:109
  196.0 5.3 %all-to-all-start.10 = ((bf16[16,16,4,512]{3,0,2,1:T(8,128)(2,1)}), bf16[16,16,4,512]{3,0,2,1:T(8,128)(2,1)}, u32[]{:S(2)}, u32[]{:S(2)}) async-start(bf16[16,16,4,512]{3,0,2,1:T(8,128)(2,1)} %bitcast.31), calls=%async_computation.10 | async-start | bytes 2097152 | tf_op jit(solution)/shard_map/all_to_all | solution.py:110
  201.4 8.3 %fusion.26 = bf16[16,512,64]{1,2,0:T(8,128)(2,1)} fusion(bf16[16,512,64]{1,2,0:T(8,128)(2,1)S(1)} %copy-done.16, f32[16,512,512]{1,2,0:T(8,128)} %get-tuple-element.23, f32[16,512]{1,0:T(8,128)S(1)} %get-tuple-element.22), kind=kOutput, calls=%fused_computation.47 | convolution fusion | flops 545783808 | bytes 18907136 | tf_op jit(solution)/shard_map/bhqk,bkhd->bqhd/dot_general | solution.py:25
  221.1 7.5 %all-to-all-start.14 = ((bf16[8,2,32768]{2,1,0:T(2,128)(2,1)}), bf16[8,2,32768]{2,1,0:T(2,128)(2,1)}, u32[]{:S(2)}, u32[]{:S(2)}) async-start(bf16[8,2,32768]{2,1,0:T(2,128)(2,1)} %reshape.160), calls=%async_computation.14 | async-start | bytes 2097152 | tf_op jit(solution)/shard_map/all_to_all | solution.py:91
  228.6 5.8 %multiply_convert_fusion.5 = bf16[16,512,64]{1,2,0:T(8,128)(2,1)} fusion(bf16[16,512,64]{1,2,0:T(8,128)(2,1)S(1)} %reshape.135, bf16[16,512,512]{1,2,0:T(8,128)(2,1)} %multiply_convert_fusion), kind=kOutput, calls=%fused_computation.39 | convolution fusion | flops 537919488 | bytes 10485760 | tf_op jit(solution)/shard_map/bhqk,bkhd->bqhd/dot_general | solution.py:30
  234.4 3.1 copy.121
  240.1 7.0 %multiply_convert_fusion.3 = bf16[16,512,64]{1,2,0:T(8,128)(2,1)} fusion(bf16[16,512,512]{1,2,0:T(8,128)(2,1)} %multiply_convert_fusion, bf16[16,512,64]{1,2,0:T(8,128)(2,1)S(1)} %copy-done.15), kind=kOutput, calls=%fused_computation.37 | convolution fusion | flops 537919488 | bytes 10485760 | tf_op jit(solution)/shard_map/bhqk,bqhd->bkhd/dot_general | solution.py:34
  262.9 6.9 %all-to-all-start.3 = ((bf16[8,2,32768]{2,1,0:T(2,128)(2,1)}), bf16[8,2,32768]{2,1,0:T(2,128)(2,1)S(1)}, u32[]{:S(2)}, u32[]{:S(2)}) async-start(bf16[8,2,32768]{2,1,0:T(2,128)(2,1)} %reshape.152), calls=%async_computation.3 | async-start | bytes 2097152 | tf_op jit(solution)/shard_map/all_to_all | solution.py:88
  269.8 4.5 fusion.38
  275.4 3.9 reshape_squeeze.14
  279.2 3.0 copy.113
  284.5 3.9 reshape_squeeze.15
  288.4 3.0 copy.125
  291.4 12.2 %fusion.50 = (f32[4,8,256]{2,1,0:T(8,128)S(1)}, f32[4,8,256,256]{2,3,1,0:T(8,128)}) fusion(f32[4,8,256,256]{2,3,1,0:T(8,128)} %fusion.38, pred[256,256]{0,1:T(8,128)(4,1)S(1)} %iota_compare_fusion.1), kind=kOutput, calls=%fused_computation.69 | output fusion | flops 12583167 | bytes 16875520 | tf_op jit(solution)/shard_map/sub | solution.py:22
  303.7 6.7 %all-to-all-start.9 = ((bf16[8,2,32768]{2,1,0:T(2,128)(2,1)}), bf16[8,2,32768]{2,1,0:T(2,128)(2,1)}, u32[]{:S(2)}, u32[]{:S(2)}) async-start(bf16[8,2,32768]{2,1,0:T(2,128)(2,1)} %reshape.156), calls=%async_computation.9 | async-start | bytes 2097152 | tf_op jit(solution)/shard_map/all_to_all | solution.py:89
  310.3 6.0 %fusion.23 = bf16[4,8,256,64]{2,3,1,0:T(8,128)(2,1)} fusion(bf16[256,4,8,64]{0,3,2,1:T(8,128)(2,1)} %copy.125, f32[4,8,256,256]{2,3,1,0:T(8,128)} %get-tuple-element.21, f32[4,8,256]{2,1,0:T(8,128)S(1)} %get-tuple-element.20), kind=kOutput, calls=%fused_computation.46 | convolution fusion | flops 273154048 | bytes 10518528 | tf_op jit(solution)/shard_map/bhqk,bqhd->bkhd/dot_general | solution.py:37
  318.9 8.8 %all-to-all-done.9 = bf16[8,2,32768]{2,1,0:T(2,128)(2,1)} async-done(((bf16[8,2,32768]{2,1,0:T(2,128)(2,1)}), bf16[8,2,32768]{2,1,0:T(2,128)(2,1)}, u32[]{:S(2)}, u32[]{:S(2)}) %all-to-all-start.9) | async-done | bytes 1048608 | tf_op jit(solution)/shard_map/all_to_all | solution.py:89
  327.7 4.2 all-to-all-start.12
  332.0 5.5 %fusion.20 = bf16[4,8,256,64]{2,3,1,0:T(8,128)(2,1)} fusion(bf16[256,4,8,64]{0,3,2,1:T(8,128)(2,1)} %copy.113, f32[4,8,256,256]{2,3,1,0:T(8,128)} %get-tuple-element.21, f32[4,8,256]{2,1,0:T(8,128)S(1)} %get-tuple-element.20), kind=kOutput, calls=%fused_computation.45 | convolution fusion | flops 273154048 | bytes 10518528 | tf_op jit(solution)/shard_map/bhqk,bkhd->bqhd/dot_general | solution.py:25
  340.1 9.2 %all-to-all-done.12 = bf16[8,2,32768]{2,1,0:T(2,128)(2,1)} async-done(((bf16[8,2,32768]{2,1,0:T(2,128)(2,1)}), bf16[8,2,32768]{2,1,0:T(2,128)(2,1)}, u32[]{:S(2)}, u32[]{:S(2)}) %all-to-all-start.12) | async-done | bytes 1048608 | tf_op jit(solution)/shard_map/all_to_all | solution.py:90
  349.3 5.7 %all-to-all-start.15 = ((bf16[256,1,4,512]{3,2,1,0:T(4,128)(2,1)}), bf16[256,1,4,512]{3,2,1,0:T(4,128)(2,1)}, u32[]{:S(2)}, u32[]{:S(2)}) async-start(bf16[256,1,4,512]{3,2,1,0:T(4,128)(2,1)} %bitcast.218), calls=%async_computation.15 | async-start | bytes 2097152 | tf_op jit(solution)/shard_map/all_to_all | solution.py:117
  355.0 8.7 %multiply_reduce_fusion.1 = (f32[4,8,256]{2,1,0:T(8,128)S(1)}, f32[4,8,256,256]{2,3,1,0:T(8,128)}) fusion(f32[4,8,256,256]{2,3,1,0:T(8,128)} %get-tuple-element.21, f32[4,8,256]{2,1,0:T(8,128)S(1)} %get-tuple-element.20, bf16[256,4,8,64]{0,3,2,1:T(8,128)(2,1)} %copy.113, bf16[256,4,8,64]{0,3,2,1:T(8,128)(2,1)} %copy.125), kind=kOutput, calls=%fused_computation.8 | convolution fusion | flops 274718720 | bytes 18939904 | tf_op jit(solution)/shard_map/bqhd,bkhd->bhqk/dot_general | solution.py:26
  363.7 7.3 %all-to-all-done.15 = bf16[256,1,4,512]{3,2,1,0:T(4,128)(2,1)} async-done(((bf16[256,1,4,512]{3,2,1,0:T(4,128)(2,1)}), bf16[256,1,4,512]{3,2,1,0:T(4,128)(2,1)}, u32[]{:S(2)}, u32[]{:S(2)}) %all-to-all-start.15) | async-done | bytes 1048608 | tf_op jit(solution)/shard_map/all_to_all | solution.py:117
  370.9 5.2 %all-to-all-start.7 = ((bf16[256,1,4,512]{3,2,1,0:T(4,128)(2,1)}), bf16[256,1,4,512]{3,2,1,0:T(4,128)(2,1)}, u32[]{:S(2)}, u32[]{:S(2)}) async-start(bf16[256,1,4,512]{3,2,1,0:T(4,128)(2,1)} %bitcast.217), calls=%async_computation.7 | async-start | bytes 2097152 | tf_op jit(solution)/shard_map/all_to_all | solution.py:114
  376.1 6.7 %multiply_convert_fusion.1 = bf16[4,8,256,256]{2,3,1,0:T(8,128)(2,1)S(1)} fusion(f32[4,8,256,256]{2,3,1,0:T(8,128)} %get-tuple-element.25, f32[4,8,256]{2,1,0:T(8,128)S(1)} %get-tuple-element.24, f32[4,8,256,256]{2,3,1,0:T(8,128)} %get-tuple-element.21, f32[4,8,256]{2,1,0:T(8,128)S(1)} %get-tuple-element.20), kind=kLoop, calls=%fused_computation.7 | loop fusion | flops 8388608 | bytes 21037056 | tf_op jit(solution)/shard_map/convert_element_type | solution.py:28
  392.2 4.2 all-to-all-start.13
  396.3 4.0 multiply_convert_fusion.4
  403.0 9.3 %all-to-all-done.13 = bf16[256,1,4,512]{3,2,1,0:T(4,128)(2,1)S(1)} async-done(((bf16[256,1,4,512]{3,2,1,0:T(4,128)(2,1)}), bf16[256,1,4,512]{3,2,1,0:T(4,128)(2,1)S(1)}, u32[]{:S(2)}, u32[]{:S(2)}) %all-to-all-start.13) | async-done | bytes 1048608 | tf_op jit(solution)/shard_map/all_to_all | solution.py:116
  413.3 4.8 all-to-all-start.11
  418.0 3.1 reshape.161
  421.1 3.8 copy.168
  424.9 4.0 all_to_all.232
  430.4 3.8 copy.172
  434.1 3.2 all_to_all.196
  437.3 3.1 reshape.157
  440.4 3.8 copy.170
  444.2 4.0 all_to_all.215
  448.2 3.2 reshape.159
  451.5 3.8 copy.169
  455.2 3.2 all_to_all.225
  (101 shorter events, 117.4 us)
Async XLA Ops:
  8.0 25.6 %all-to-all-start = ((bf16[8,2,32768]{2,1,0:T(2,128)(2,1)}), bf16[8,2,32768]{2,1,0:T(2,128)(2,1)S(1)}, u32[]{:S(2)}, u32[]{:S(2)}) async-start(bf16[8,2,32768]{2,1,0:T(2,128)(2,1)} %reshape.148), calls=%async_computation | async-start | bytes 2097152 | tf_op jit(solution)/shard_map/all_to_all | solution.py:81
  33.7 21.6 %all-to-all-start.1 = ((bf16[8,2,32768]{2,1,0:T(2,128)(2,1)}), bf16[8,2,32768]{2,1,0:T(2,128)(2,1)}, u32[]{:S(2)}, u32[]{:S(2)}) async-start(bf16[8,2,32768]{2,1,0:T(2,128)(2,1)} %reshape.150), calls=%async_computation.1 | async-start | bytes 2097152 | tf_op jit(solution)/shard_map/all_to_all | solution.py:82
  55.3 21.6 %all-to-all-start.2 = ((bf16[8,2,32768]{2,1,0:T(2,128)(2,1)}), bf16[8,2,32768]{2,1,0:T(2,128)(2,1)}, u32[]{:S(2)}, u32[]{:S(2)}) async-start(bf16[8,2,32768]{2,1,0:T(2,128)(2,1)} %reshape.146), calls=%async_computation.2 | async-start | bytes 2097152 | tf_op jit(solution)/shard_map/all_to_all | solution.py:83
  68.2 15.9 %copy-start.9 = (bf16[16,64,512]{2,1,0:T(8,128)(2,1)S(1)}, bf16[16,64,512]{2,1,0:T(8,128)(2,1)}, u32[]{:S(2)}) copy-start(bf16[16,64,512]{2,1,0:T(8,128)(2,1)} %get-tuple-element.15) | copy-start | bytes 3145732
  68.3 17.5 %copy-start.10 = (bf16[16,64,512]{2,1,0:T(8,128)(2,1)S(1)}, bf16[16,64,512]{2,1,0:T(8,128)(2,1)}, u32[]{:S(2)}) copy-start(bf16[16,64,512]{2,1,0:T(8,128)(2,1)} %get-tuple-element.19) | copy-start | bytes 3145732
  76.9 39.0 %all-to-all-start.8 = ((bf16[8,2,32768]{2,1,0:T(2,128)(2,1)}), bf16[8,2,32768]{2,1,0:T(2,128)(2,1)}, u32[]{:S(2)}, u32[]{:S(2)}) async-start(bf16[8,2,32768]{2,1,0:T(2,128)(2,1)} %reshape.154), calls=%async_computation.8 | async-start | bytes 2097152 | tf_op jit(solution)/shard_map/all_to_all | solution.py:84
  81.3 6.0 %copy-start.12 = (bf16[16,64,512]{2,1,0:T(8,128)(2,1)S(1)}, bf16[16,64,512]{2,1,0:T(8,128)(2,1)}, u32[]{:S(2)}) copy-start(bf16[16,64,512]{2,1,0:T(8,128)(2,1)} %get-tuple-element.13) | copy-start | bytes 3145732
  115.9 36.7 %all-to-all-start.4 = ((bf16[16,16,4,512]{3,0,2,1:T(8,128)(2,1)}), bf16[16,16,4,512]{3,0,2,1:T(8,128)(2,1)}, u32[]{:S(2)}, u32[]{:S(2)}) async-start(bf16[16,16,4,512]{3,0,2,1:T(8,128)(2,1)} %bitcast.216), calls=%async_computation.4 | async-start | bytes 2097152 | tf_op jit(solution)/shard_map/all_to_all | solution.py:107
  130.9 11.0 %copy-start.17 = (bf16[16,512,64]{1,2,0:T(8,128)(2,1)}, bf16[16,512,64]{1,2,0:T(8,128)(2,1)S(1)}, u32[]{:S(2)}) copy-start(bf16[16,512,64]{1,2,0:T(8,128)(2,1)S(1)} %reshape.141) | copy-start | bytes 3145732
  130.9 11.0 %copy-start.16 = (bf16[16,512,64]{1,2,0:T(8,128)(2,1)S(1)}, bf16[16,512,64]{1,2,0:T(8,128)(2,1)}, u32[]{:S(2)}) copy-start(bf16[16,512,64]{1,2,0:T(8,128)(2,1)} %reshape.136) | copy-start | bytes 3145732
  152.6 21.6 %all-to-all-start.5 = ((bf16[16,16,4,512]{3,0,2,1:T(8,128)(2,1)}), bf16[16,16,4,512]{3,0,2,1:T(8,128)(2,1)S(1)}, u32[]{:S(2)}, u32[]{:S(2)}) async-start(bf16[16,16,4,512]{3,0,2,1:T(8,128)(2,1)} %bitcast.12), calls=%async_computation.5 | async-start | bytes 2097152 | tf_op jit(solution)/shard_map/all_to_all | solution.py:108
  174.2 1.0 copy-start.3
  175.1 20.9 %all-to-all-start.6 = ((bf16[16,16,4,512]{3,0,2,1:T(8,128)(2,1)}), bf16[16,16,4,512]{3,0,2,1:T(8,128)(2,1)S(1)}, u32[]{:S(2)}, u32[]{:S(2)}) async-start(bf16[16,16,4,512]{3,0,2,1:T(8,128)(2,1)} %bitcast.16), calls=%async_computation.6 | async-start | bytes 2097152 | tf_op jit(solution)/shard_map/all_to_all | solution.py:109
  196.0 5.4 %copy-start.1 = (bf16[16,16,4,512]{3,0,2,1:T(8,128)(2,1)}, bf16[16,16,4,512]{3,0,2,1:T(8,128)(2,1)S(1)}, u32[]{:S(2)}) copy-start(bf16[16,16,4,512]{3,0,2,1:T(8,128)(2,1)S(1)} %all-to-all-done.6) | copy-start | bytes 3145732
  196.0 25.0 %all-to-all-start.10 = ((bf16[16,16,4,512]{3,0,2,1:T(8,128)(2,1)}), bf16[16,16,4,512]{3,0,2,1:T(8,128)(2,1)}, u32[]{:S(2)}, u32[]{:S(2)}) async-start(bf16[16,16,4,512]{3,0,2,1:T(8,128)(2,1)} %bitcast.31), calls=%async_computation.10 | async-start | bytes 2097152 | tf_op jit(solution)/shard_map/all_to_all | solution.py:110
  221.1 41.8 %all-to-all-start.14 = ((bf16[8,2,32768]{2,1,0:T(2,128)(2,1)}), bf16[8,2,32768]{2,1,0:T(2,128)(2,1)}, u32[]{:S(2)}, u32[]{:S(2)}) async-start(bf16[8,2,32768]{2,1,0:T(2,128)(2,1)} %reshape.160), calls=%async_computation.14 | async-start | bytes 2097152 | tf_op jit(solution)/shard_map/all_to_all | solution.py:91
  234.4 5.8 %copy-start.15 = (bf16[16,512,64]{1,2,0:T(8,128)(2,1)S(1)}, bf16[16,512,64]{1,2,0:T(8,128)(2,1)}, u32[]{:S(2)}) copy-start(bf16[16,512,64]{1,2,0:T(8,128)(2,1)} %reshape.134) | copy-start | bytes 3145732
  252.8 5.7 %copy-start.4 = (bf16[16,16,4,512]{3,0,2,1:T(8,128)(2,1)S(1)}, bf16[16,16,4,512]{3,0,2,1:T(8,128)(2,1)}, u32[]{:S(2)}) copy-start(bf16[16,16,4,512]{3,0,2,1:T(8,128)(2,1)} %copy-done.3) | copy-start | bytes 3145732
  262.9 40.8 %all-to-all-start.3 = ((bf16[8,2,32768]{2,1,0:T(2,128)(2,1)}), bf16[8,2,32768]{2,1,0:T(2,128)(2,1)S(1)}, u32[]{:S(2)}, u32[]{:S(2)}) async-start(bf16[8,2,32768]{2,1,0:T(2,128)(2,1)} %reshape.152), calls=%async_computation.3 | async-start | bytes 2097152 | tf_op jit(solution)/shard_map/all_to_all | solution.py:88
  269.8 4.6 copy-start.2
  303.7 24.1 %all-to-all-start.9 = ((bf16[8,2,32768]{2,1,0:T(2,128)(2,1)}), bf16[8,2,32768]{2,1,0:T(2,128)(2,1)}, u32[]{:S(2)}, u32[]{:S(2)}) async-start(bf16[8,2,32768]{2,1,0:T(2,128)(2,1)} %reshape.156), calls=%async_computation.9 | async-start | bytes 2097152 | tf_op jit(solution)/shard_map/all_to_all | solution.py:89
  327.7 21.6 %all-to-all-start.12 = ((bf16[8,2,32768]{2,1,0:T(2,128)(2,1)}), bf16[8,2,32768]{2,1,0:T(2,128)(2,1)}, u32[]{:S(2)}, u32[]{:S(2)}) async-start(bf16[8,2,32768]{2,1,0:T(2,128)(2,1)} %reshape.158), calls=%async_computation.12 | async-start | bytes 2097152 | tf_op jit(solution)/shard_map/all_to_all | solution.py:90
  349.3 21.6 %all-to-all-start.15 = ((bf16[256,1,4,512]{3,2,1,0:T(4,128)(2,1)}), bf16[256,1,4,512]{3,2,1,0:T(4,128)(2,1)}, u32[]{:S(2)}, u32[]{:S(2)}) async-start(bf16[256,1,4,512]{3,2,1,0:T(4,128)(2,1)} %bitcast.218), calls=%async_computation.15 | async-start | bytes 2097152 | tf_op jit(solution)/shard_map/all_to_all | solution.py:117
  370.9 21.3 %all-to-all-start.7 = ((bf16[256,1,4,512]{3,2,1,0:T(4,128)(2,1)}), bf16[256,1,4,512]{3,2,1,0:T(4,128)(2,1)}, u32[]{:S(2)}, u32[]{:S(2)}) async-start(bf16[256,1,4,512]{3,2,1,0:T(4,128)(2,1)} %bitcast.217), calls=%async_computation.7 | async-start | bytes 2097152 | tf_op jit(solution)/shard_map/all_to_all | solution.py:114
  382.8 2.0 copy-start
  392.2 20.1 %all-to-all-start.13 = ((bf16[256,1,4,512]{3,2,1,0:T(4,128)(2,1)}), bf16[256,1,4,512]{3,2,1,0:T(4,128)(2,1)S(1)}, u32[]{:S(2)}, u32[]{:S(2)}) async-start(bf16[256,1,4,512]{3,2,1,0:T(4,128)(2,1)} %bitcast.219), calls=%async_computation.13 | async-start | bytes 2097152 | tf_op jit(solution)/shard_map/all_to_all | solution.py:116
  412.3 1.0 copy-start.5
  413.3 51.5 %all-to-all-start.11 = ((bf16[256,1,4,512]{3,2,1,0:T(4,128)(2,1)}), bf16[256,1,4,512]{3,2,1,0:T(4,128)(2,1)}, u32[]{:S(2)}, u32[]{:S(2)}) async-start(bf16[256,1,4,512]{3,2,1,0:T(4,128)(2,1)} %bitcast.38), calls=%async_computation.11 | async-start | bytes 2097152 | tf_op jit(solution)/shard_map/all_to_all | solution.py:115
  458.4 5.1 %copy-start.6 = (bf16[256,1,4,512]{3,2,1,0:T(4,128)(2,1)S(1)}, bf16[256,1,4,512]{3,2,1,0:T(4,128)(2,1)}, u32[]{:S(2)}) copy-start(bf16[256,1,4,512]{3,2,1,0:T(4,128)(2,1)} %copy-done.5) | copy-start | bytes 3145732
  463.5 2.9 copy-start.7
  464.8 1.6 copy-start.14
  466.4 2.8 copy-start.13
  469.2 2.8 copy-start.8
  472.0 2.8 copy-start.11
where the time goes:
time: 485 us; the launch traced here: 478 us
  local copies, waits for them, and re-layouts  200 us (41%)
  starting transfers between devices  88.3 us (18%)
  matrix products  83.6 us (17%)
  waiting for transfers between devices  69.7 us (14%)
  other arithmetic  35.3 us (7%)
    unnamed x60, local copies, waits for them, and re-layouts  67.8 us
    another operation x8, local copies, waits for them, and re-layouts, split_heads(): array.reshape(array.shape[:-1] + (array.shape[-1] // HEAD_DIM, HEAD_DIM))  22.4 us
    convert_element_type x2, other arithmetic, attend(): dscores = (probs * (dprobs - row_delta)).astype(jnp.bfloat16)  21.9 us
    dot_general x2, matrix products, attend(): jnp.einsum('bqhd,bkhd->bhqk', grad_out, value, preferred_element_type=jnp...  19.4 us
    dot_general x2, matrix products, attend(): jnp.einsum('bhqk,bqhd->bkhd', probs_low, grad_out, preferred_element_type...  15.6 us
    another operation x4, local copies, waits for them, and re-layouts  14.5 us
    dot_general x2, matrix products, attend(): jnp.einsum('bhqk,bkhd->bqhd', probs_low, value, preferred_element_type=jn...  13.9 us
    sub x1, other arithmetic, attend(): weights = jnp.exp(scores - row_max)  12.2 us
  transfers between devices with their start and end apart: 16, of which 10 were waited for; matrix products, arithmetic and copies ran while one was open for 59% of the time, Pallas kernels for 0%

commit v1 on v0

v1 whole, which is shorter than its diff:
```python
import functools

import jax
import jax.numpy as jnp
from jax import lax
from jax.experimental import pallas as pl
from jax.experimental.pallas import tpu as pltpu
from jax.sharding import PartitionSpec as P

MESH = pl.DeviceIdType.MESH
STEPS = 4
LANES = 128
HALF = 512
ROWS_HERE = 16
COLS_HERE = 64
ROW_SEQ = 256
COL_SEQ = 128
COL_BLOCK = 32
ROW_STEP = ROWS_HERE // STEPS
COL_STEP = COL_BLOCK // STEPS
NT = (((1,), (1,)), ((), ()))
TN = (((0,), (0,)), ((), ()))
NN = (((1,), (0,)), ((), ()))


def dot(a, b, dims):
    return lax.dot_general(a, b, dims, preferred_element_type=jnp.float32)


def attend(q, k, v, g, k_low, v_low):
    length = q.shape[0]
    lane = lax.broadcasted_iota(jnp.int32, (1, LANES), 1)
    allowed = lax.broadcasted_iota(jnp.int32, (length, length), 1) <= lax.broadcasted_iota(
        jnp.int32, (length, length), 0
    )
    zero = jnp.zeros((), jnp.bfloat16)
    q = q * jnp.bfloat16(0.125)
    totals = None
    for head in range(2):
        mine = (lane < 64) if head == 0 else (lane >= 64)
        qh, kh, vh, gh = [jnp.where(mine, t, zero) for t in (q, k, v, g)]
        scores = jnp.where(allowed, dot(qh, k, NT), -1e30)
        dprobs = dot(gh, v, NT)
        top = jnp.max(scores, axis=1, keepdims=True)
        if k_low is not None:
            scores_low = dot(qh, k_low, NT)
            dprobs_low = dot(gh, v_low, NT)
            top = jnp.maximum(top, jnp.max(scores_low, axis=1, keepdims=True))
        weights = jnp.exp(scores - top)
        norm = jnp.sum(weights, axis=1, keepdims=True)
        if k_low is not None:
            weights_low = jnp.exp(scores_low - top)
            norm = norm + jnp.sum(weights_low, axis=1, keepdims=True)
        inverse = 1.0 / norm
        probs = weights * inverse
        delta = jnp.sum(probs * dprobs, axis=1, keepdims=True)
        if k_low is not None:
            probs_low = weights_low * inverse
            delta = delta + jnp.sum(probs_low * dprobs_low, axis=1, keepdims=True)
        ds = (probs * (dprobs - delta)).astype(jnp.bfloat16)
        pb = probs.astype(jnp.bfloat16)
        parts = [dot(pb, vh, NN), dot(ds, kh, NN), dot(ds, qh, TN), dot(pb, gh, TN)]
        if k_low is not None:
            ds_low = (probs_low * (dprobs_low - delta)).astype(jnp.bfloat16)
            pb_low = probs_low.astype(jnp.bfloat16)
            kh_low, vh_low = [jnp.where(mine, t, zero) for t in (k_low, v_low)]
            parts[0] = parts[0] + dot(pb_low, vh_low, NN)
            parts[1] = parts[1] + dot(ds_low, kh_low, NN)
            parts += [dot(ds_low, qh, TN), dot(pb_low, gh, TN)]
        totals = parts if totals is None else [a + b for a, b in zip(totals, parts)]
    totals[1] = totals[1] * 0.125
    return totals


def body(
    q_ref, k_ref, v_ref, g_ref, raw_row, raw_col,
    row_in, row_low, row_out, row_part, row_keep,
    col_in, col_low, col_out, col_part, col_keep,
    stage, send,
    ri_s, ri_r, ri_l, ci_s, ci_r, ci_l,
    ro_s, ro_r, ro_l, co_s, co_r, co_l,
    rf_s, rf_r, cf_s, cf_r, st_l,
):
    inputs = (q_ref, k_ref, v_ref, g_ref)
    row, col = lax.axis_index("row"), lax.axis_index("col")
    z_lo, xc = row // 8, row % 8
    x, core = xc // 2, xc % 2
    z_hi, y = col // 4, col % 4

    def row_peer(d):
        other = (y + d) % 4
        return other, (row, z_hi * 4 + other)

    def col_peer(d):
        other = (xc + d) % 8
        return other, (z_lo * 8 + other, col)

    row_partner = (row, (1 - z_hi) * 4 + y)
    col_partner = ((1 - z_lo) * 8 + xc, col)

    for a in range(4):
        pltpu.make_async_copy(inputs[a].at[:, :, pl.ds(HALF, HALF)], stage.at[a], st_l.at[a]).start()

    barrier = pltpu.get_barrier_semaphore()
    everyone = [row_peer(d)[1] for d in range(1, 4)] + [col_peer(d)[1] for d in range(1, 8)]
    everyone += [row_partner, col_partner]
    for device in everyone:
        pl.semaphore_signal(barrier, inc=1, device_id=device, device_id_type=MESH)
    pl.semaphore_wait(barrier, len(everyone))

    def lanes(i):
        return pl.ds(pl.multiple_of(i * LANES, LANES), LANES)

    def row_in_copy(i, a, d):
        other, device = row_peer(d)
        return pltpu.make_async_remote_copy(
            inputs[a].at[pl.ds(i * ROW_STEP, ROW_STEP), :, lanes(other)],
            row_in.at[a, pl.ds(i * ROW_STEP, ROW_STEP), pl.ds(y * COLS_HERE, COLS_HERE)],
            ri_s.at[i, a, d - 1], ri_r.at[i, a, d - 1], device_id=device, device_id_type=MESH,
        )

    def row_in_own(i, a):
        return pltpu.make_async_copy(
            inputs[a].at[pl.ds(i * ROW_STEP, ROW_STEP), :, lanes(y)],
            row_in.at[a, pl.ds(i * ROW_STEP, ROW_STEP), pl.ds(y * COLS_HERE, COLS_HERE)],
            ri_l.at[i, a],
        )

    def row_in_arrival(i, a, d):
        src = (y + 4 - d) % 4
        place = row_in.at[a, pl.ds(i * ROW_STEP, ROW_STEP), pl.ds(src * COLS_HERE, COLS_HERE)]
        return pltpu.make_async_remote_copy(
            place, place, ri_s.at[i, a, d - 1], ri_r.at[i, a, d - 1],
            device_id=row_peer(d)[1], device_id_type=MESH,
        )

    def col_in_copy(i, d):
        other, device = col_peer(d)
        return pltpu.make_async_remote_copy(
            send.at[:, pl.ds((other % 2) * COL_BLOCK + i * COL_STEP, COL_STEP), :, lanes(other // 2)],
            col_in.at[:, pl.ds(i * COL_STEP, COL_STEP), pl.ds(xc * ROWS_HERE, ROWS_HERE)],
            ci_s.at[i, d - 1], ci_r.at[i, d - 1], device_id=device, device_id_type=MESH,
        )

    def col_in_own(i):
        return pltpu.make_async_copy(
            send.at[:, pl.ds(core * COL_BLOCK + i * COL_STEP, COL_STEP), :, lanes(x)],
            col_in.at[:, pl.ds(i * COL_STEP, COL_STEP), pl.ds(xc * ROWS_HERE, ROWS_HERE)],
            ci_l.at[i],
        )

    def col_in_arrival(i, d):
        src = (xc + 8 - d) % 8
        place = col_in.at[:, pl.ds(i * COL_STEP, COL_STEP), pl.ds(src * ROWS_HERE, ROWS_HERE)]
        return pltpu.make_async_remote_copy(
            place, place, ci_s.at[i, d - 1], ci_r.at[i, d - 1],
            device_id=col_peer(d)[1], device_id_type=MESH,
        )

    def row_out_copy(i, part, d):
        other, device = row_peer(d)
        return pltpu.make_async_remote_copy(
            row_out.at[pl.ds(2 * part, 2), pl.ds(i * ROW_STEP, ROW_STEP), pl.ds(other * COLS_HERE, COLS_HERE)],
            raw_row.at[pl.ds(2 * part, 2), pl.ds(i * ROW_STEP, ROW_STEP), :, lanes(y)],
            ro_s.at[i, part, d - 1], ro_r.at[i, part, d - 1], device_id=device, device_id_type=MESH,
        )

    def row_out_own(i, part):
        return pltpu.make_async_copy(
            row_out.at[pl.ds(2 * part, 2), pl.ds(i * ROW_STEP, ROW_STEP), pl.ds(y * COLS_HERE, COLS_HERE)],
            raw_row.at[pl.ds(2 * part, 2), pl.ds(i * ROW_STEP, ROW_STEP), :, lanes(y)],
            ro_l.at[i, part],
        )

    def row_out_arrival(i, part, d):
        src = (y + 4 - d) % 4
        place = raw_row.at[pl.ds(2 * part, 2), pl.ds(i * ROW_STEP, ROW_STEP), :, lanes(src)]
        return pltpu.make_async_remote_copy(
            place, place, ro_s.at[i, part, d - 1], ro_r.at[i, part, d - 1],
            device_id=row_peer(d)[1], device_id_type=MESH,
        )

    def col_out_copy(i, part, d):
        other, device = col_peer(d)
        return pltpu.make_async_remote_copy(
            col_out.at[pl.ds(2 * part, 2), pl.ds(i * COL_STEP, COL_STEP), pl.ds(other * ROWS_HERE, ROWS_HERE)],
            raw_col.at[pl.ds(2 * part, 2), pl.ds(core * COL_BLOCK + i * COL_STEP, COL_STEP), :, lanes(x)],
            co_s.at[i, part, d - 1], co_r.at[i, part, d - 1], device_id=device, device_id_type=MESH,
        )

    def col_out_own(i, part):
        return pltpu.make_async_copy(
            col_out.at[pl.ds(2 * part, 2), pl.ds(i * COL_STEP, COL_STEP), pl.ds(xc * ROWS_HERE, ROWS_HERE)],
            raw_col.at[pl.ds(2 * part, 2), pl.ds(core * COL_BLOCK + i * COL_STEP, COL_STEP), :, lanes(x)],
            co_l.at[i, part],
        )

    def col_out_arrival(i, part, d):
        src = (xc + 8 - d) % 8
        place = raw_col.at[
            pl.ds(2 * part, 2), pl.ds((src % 2) * COL_BLOCK + i * COL_STEP, COL_STEP), :, lanes(src // 2)
        ]
        return pltpu.make_async_remote_copy(
            place, place, co_s.at[i, part, d - 1], co_r.at[i, part, d - 1],
            device_id=col_peer(d)[1], device_id_type=MESH,
        )

    def half_copy(i, upper, source, low, step, partner, s_sem, r_sem):
        return pltpu.make_async_remote_copy(
            source.at[pl.ds(0 if upper else 1, 2), pl.ds(i * step, step)],
            low.at[:, pl.ds(i * step, step)],
            s_sem.at[i], r_sem.at[i], device_id=partner, device_id_type=MESH,
        )

    row_half = functools.partial(half_copy, low=row_low, step=ROW_STEP, partner=row_partner, s_sem=rf_s, r_sem=rf_r)
    col_half = functools.partial(half_copy, low=col_low, step=COL_STEP, partner=col_partner, s_sem=cf_s, r_sem=cf_r)

    def issue_row(i, carry):
        for a in (1, 2, 0, 3):
            for d in (2, 1, 3):
                row_in_copy(i, a, d).start()
            row_in_own(i, a).start()
        return carry

    issue_row(0, 0)

    to = lax.broadcasted_iota(jnp.int32, (256, 256), 0)
    frm = lax.broadcasted_iota(jnp.int32, (256, 256), 1)
    turn = jnp.where(frm == (to % 16) * 16 + to // 16, 1.0, 0.0).astype(jnp.bfloat16)

    def turn_blocks(part):
        def one(t, carry):
            a, at = t // 2, (t % 2) * COL_BLOCK + part * 16
            block = stage[a, :, pl.ds(pl.multiple_of(at, 16), 16), :].reshape(256, HALF)
            turned = dot(turn, block, NN).astype(jnp.bfloat16).reshape(16, 16, HALF)
            send[a, pl.ds(at, 16)] = turned
            return carry

        lax.fori_loop(0, 8, one, 0)
        for j in range(STEPS // 2):
            i = part * (STEPS // 2) + j
            for d in (4, 5, 2, 3, 6, 7, 1):
                col_in_copy(i, d).start()
            col_in_own(i).start()

    for a in range(4):
        pltpu.make_async_copy(inputs[a].at[:, :, pl.ds(HALF, HALF)], stage.at[a], st_l.at[a]).wait()
    turn_blocks(0)
    lax.fori_loop(1, STEPS // 2, issue_row, 0)
    turn_blocks(1)
    lax.fori_loop(STEPS // 2, STEPS, issue_row, 0)

    def send_row(i, part):
        for d in (2, 1, 3):
            row_out_copy(i, part, d).start()
        row_out_own(i, part).start()

    def send_col(i, part):
        for d in (4, 5, 2, 3, 6, 7, 1):
            col_out_copy(i, part, d).start()
        col_out_own(i, part).start()

    def work(upper, box, low, out, part, keep, step, i):
        def one(n, carry):
            q, k, v, g = [box[a, n] for a in range(4)]
            if upper:
                found = attend(q, k, v, g, low[0, n], low[1, n])
                for a in range(4):
                    out[a, n] = found[a].astype(jnp.bfloat16)
                part[0, n] = found[4].astype(jnp.bfloat16)
                part[1, n] = found[5].astype(jnp.bfloat16)
            else:
                found = attend(q, k, v, g, None, None)
                out[0, n] = found[0].astype(jnp.bfloat16)
                out[1, n] = found[1].astype(jnp.bfloat16)
                keep[0, n] = found[2]
                keep[1, n] = found[3]
            return carry

        lax.fori_loop(i * step, (i + 1) * step, one, 0)

    def finish(half, low, out, keep, step, i):
        half(i, True, low).wait_recv()

        def one(n, carry):
            for a in range(2):
                out[2 + a, n] = (keep[a, n] + low[a, n].astype(jnp.float32)).astype(jnp.bfloat16)
            return carry

        lax.fori_loop(i * step, (i + 1) * step, one, 0)

    def row_step(i):
        for a in (1, 2, 0, 3):
            for d in range(1, 4):
                row_in_arrival(i, a, d).wait_recv()
            row_in_own(i, a).wait()

        @pl.when(z_hi == 0)
        def _():
            row_half(i, False, row_in).start()
            work(False, row_in, row_low, row_out, row_part, row_keep, ROW_STEP, i)
            send_row(i, 0)

        @pl.when(z_hi == 1)
        def _():
            row_half(i, True, row_part).wait_recv()
            work(True, row_in, row_low, row_out, row_part, row_keep, ROW_STEP, i)
            row_half(i, True, row_part).start()
            send_row(i, 0)
            send_row(i, 1)

    def col_step(i):
        for d in range(1, 8):
            col_in_arrival(i, d).wait_recv()
        col_in_own(i).wait()

        @pl.when(z_lo == 0)
        def _():
            col_half(i, False, col_in).start()
            work(False, col_in, col_low, col_out, col_part, col_keep, COL_STEP, i)
            send_col(i, 0)

        @pl.when(z_lo == 1)
        def _():
            col_half(i, True, col_part).wait_recv()
            work(True, col_in, col_low, col_out, col_part, col_keep, COL_STEP, i)
            col_half(i, True, col_part).start()
            send_col(i, 0)
            send_col(i, 1)

    def row_finish(i):
        @pl.when(z_hi == 0)
        def _():
            finish(row_half, row_low, row_out, row_keep, ROW_STEP, i)
            send_row(i, 1)

    def col_finish(i):
        @pl.when(z_lo == 0)
        def _():
            finish(col_half, col_low, col_out, col_keep, COL_STEP, i)
            send_col(i, 1)

    def step(i, carry):
        row_step(i)
        col_step(i)

        @pl.when(i > 0)
        def _():
            row_finish(i - 1)
            col_finish(i - 1)

        return carry

    lax.fori_loop(0, STEPS, step, 0)
    row_finish(STEPS - 1)
    col_finish(STEPS - 1)

    def drain(i, carry):
        for a in range(4):
            for d in range(1, 4):
                row_in_copy(i, a, d).wait_send()
        for d in range(1, 8):
            col_in_copy(i, d).wait_send()
        for part in range(2):
            for d in range(1, 4):
                row_out_copy(i, part, d).wait_send()
            for d in range(1, 8):
                col_out_copy(i, part, d).wait_send()
        row_half(i, True, row_part).wait_send()
        col_half(i, True, col_part).wait_send()
        for part in range(2):
            row_out_own(i, part).wait()
            col_out_own(i, part).wait()
            for d in range(1, 4):
                row_out_arrival(i, part, d).wait_recv()
            for d in range(1, 8):
                col_out_arrival(i, part, d).wait_recv()
        return carry

    lax.fori_loop(0, STEPS, drain, 0)


def exchange(queries, keys, values, grad_output):
    bf16, f32 = jnp.bfloat16, jnp.float32
    dma = pltpu.SemaphoreType.DMA

    def side(many, length):
        return [
            pltpu.VMEM((4, many, length, LANES), bf16),
            pltpu.VMEM((2, many, length, LANES), bf16),
            pltpu.VMEM((4, many, length, LANES), bf16),
            pltpu.VMEM((2, many, length, LANES), bf16),
            pltpu.VMEM((2, many, length, LANES), f32),
        ]

    return pl.pallas_call(
        body,
        out_shape=[
            jax.ShapeDtypeStruct((4, ROWS_HERE, COLS_HERE, HALF), bf16),
            jax.ShapeDtypeStruct((4, COLS_HERE, ROWS_HERE, HALF), bf16),
        ],
        in_specs=[pl.BlockSpec(memory_space=pl.ANY)] * 4,
        out_specs=[pl.BlockSpec(memory_space=pl.ANY)] * 2,
        scratch_shapes=side(ROWS_HERE, ROW_SEQ)
        + side(COL_BLOCK, COL_SEQ)
        + [pltpu.VMEM((4, ROWS_HERE, COLS_HERE, HALF), bf16), pltpu.VMEM((4, COLS_HERE, ROWS_HERE, HALF), bf16)]
        + [dma((STEPS, 4, 3)), dma((STEPS, 4, 3)), dma((STEPS, 4))]
        + [dma((STEPS, 7)), dma((STEPS, 7)), dma((STEPS,))]
        + [dma((STEPS, 2, 3)), dma((STEPS, 2, 3)), dma((STEPS, 2))]
        + [dma((STEPS, 2, 7)), dma((STEPS, 2, 7)), dma((STEPS, 2))]
        + [dma((STEPS,))] * 4
        + [dma((4,))],
        compiler_params=pltpu.CompilerParams(
            collective_id=0, has_side_effects=True, vmem_limit_bytes=60 * 2**20
        ),
        name="exchange",
    )(queries, keys, values, grad_output)


def join_body(row_ref, col_ref, *outs):
    to = lax.broadcasted_iota(jnp.int32, (256, 256), 0)
    frm = lax.broadcasted_iota(jnp.int32, (256, 256), 1)
    turn = jnp.where(frm == (to % 16) * 16 + to // 16, 1.0, 0.0).astype(jnp.bfloat16)
    for a in range(4):
        outs[a][:, :, :HALF] = row_ref[a]
        turned = dot(turn, col_ref[a].reshape(256, HALF), NN)
        outs[a][:, :, HALF:] = turned.astype(jnp.bfloat16).reshape(16, 16, HALF)


def join(raw_row, raw_col):
    shape = jax.ShapeDtypeStruct((ROWS_HERE, COLS_HERE, 2 * HALF), jnp.bfloat16)
    return pl.pallas_call(
        join_body,
        grid=(COLS_HERE // 16,),
        out_shape=[shape] * 4,
        in_specs=[
            pl.BlockSpec((4, ROWS_HERE, 16, HALF), lambda i: (0, 0, i, 0)),
            pl.BlockSpec((4, 16, ROWS_HERE, HALF), lambda i: (0, i, 0, 0)),
        ],
        out_specs=[pl.BlockSpec((ROWS_HERE, 16, 2 * HALF), lambda i: (0, i, 0))] * 4,
        compiler_params=pltpu.CompilerParams(vmem_limit_bytes=48 * 2**20),
        name="join",
    )(raw_row, raw_col)


def on_device(queries, keys, values, grad_output):
    raw_row, raw_col = exchange(queries, keys, values, grad_output)
    return tuple(join(raw_row, raw_col))


def solution(mesh):
    spec = P("row", "col", None)
    return jax.shard_map(
        on_device, mesh=mesh, in_specs=(spec,) * 4, out_specs=(spec,) * 4, check_vma=False
    )
```

time: 485 us -> 169 us (0.35)
  the two profiles are of different devices: /device:TPU:1 before, /device:TPU:65 now
where the time goes in v1:
time: 169 us
  Pallas kernels  166 us (98%)
  local copies, waits for them, and re-layouts  2.18 us (1%)
    pallas_call x1, Pallas kernels, exchange(): pl.pallas_call(body, out_shape=[jax.ShapeDtypeStruct((4, ROWS_HERE, COLS_...  159 us
    pallas_call x1, Pallas kernels, join(): pl.pallas_call(join_body, grid=(COLS_HERE // 16,), out_shape=[shape] * 4,...  6.78 us

profile of v1, /device:TPU:65, one launch (start us, length us, event | category | flops | bytes accessed | tf_op | source)
XLA Modules:
  0.0 168.9 jit_solution(5862142916791958801)
XLA Ops:
  0.6 159.3 %exchange.1 = (bf16[4,16,64,512]{3,2,1,0:T(8,128)(2,1)}, bf16[4,64,16,512]{3,2,1,0:T(8,128)(2,1)}) custom-call(bf16[16,64,1024]{2,1,0:T(8,128)(2,1)} %q_ref.1, bf16[16,64,1024]{2,1,0:T(8,128)(2,1)} %k_ref.1, bf16[16,64,1024]{2,1,0:T(8,128)(2,1)} %v_ref.1, bf16[16,64,1024]{2,1,0:T(8,128)(2,1)} %g_ref.1), custom_call_target="tpu_custom_call" | custom-call | tf_op jit(solution)/shard_map/exchange/pallas_call | solution.py:396
  159.9 0.0 copy-start
  159.9 2.2 %copy-done = bf16[4,16,64,512]{3,2,1,0:T(8,128)(2,1)S(1)} copy-done((bf16[4,16,64,512]{3,2,1,0:T(8,128)(2,1)S(1)}, bf16[4,16,64,512]{3,2,1,0:T(8,128)(2,1)}, u32[]{:S(2)}) %copy-start) | copy-done | bytes 4194328
  162.1 6.8 %join.1 = (bf16[16,64,1024]{2,1,0:T(8,128)(2,1)}, bf16[16,64,1024]{2,1,0:T(8,128)(2,1)}, bf16[16,64,1024]{2,1,0:T(8,128)(2,1)}, bf16[16,64,1024]{2,1,0:T(8,128)(2,1)}) custom-call(bf16[4,16,64,512]{3,2,1,0:T(8,128)(2,1)S(1)} %copy-done, bf16[4,64,16,512]{3,2,1,0:T(8,128)(2,1)} %get-tuple-element.7.col_ref), custom_call_target="tpu_custom_call" | custom-call | tf_op jit(solution)/shard_map/join/pallas_call | solution.py:432
Async XLA Ops:
  159.9 2.2 %copy-start = (bf16[4,16,64,512]{3,2,1,0:T(8,128)(2,1)S(1)}, bf16[4,16,64,512]{3,2,1,0:T(8,128)(2,1)}, u32[]{:S(2)}) copy-start(bf16[4,16,64,512]{3,2,1,0:T(8,128)(2,1)} %get-tuple-element.6.row_ref) | copy-start | bytes 12582916

commit v2 on v1

--- a/solution.py
+++ b/solution.py
@@ -8,7 +8,8 @@
 from jax.sharding import PartitionSpec as P
 
 MESH = pl.DeviceIdType.MESH
-STEPS = 4
+STEPS = 8
+LAG = 3
 LANES = 128
 HALF = 512
 ROWS_HERE = 16
@@ -18,6 +19,8 @@
 COL_BLOCK = 32
 ROW_STEP = ROWS_HERE // STEPS
 COL_STEP = COL_BLOCK // STEPS
+ROW_UNROLL = min(ROW_STEP, 2)
+COL_UNROLL = min(COL_STEP, 4)
 NT = (((1,), (1,)), ((), ()))
 TN = (((0,), (0,)), ((), ()))
 NN = (((1,), (0,)), ((), ()))
@@ -29,47 +32,67 @@
 
 def attend(q, k, v, g, k_low, v_low):
     length = q.shape[0]
-    lane = lax.broadcasted_iota(jnp.int32, (1, LANES), 1)
-    allowed = lax.broadcasted_iota(jnp.int32, (length, length), 1) <= lax.broadcasted_iota(
-        jnp.int32, (length, length), 0
+    keys_at = lax.broadcasted_iota(jnp.int32, (length, 2 * length), 0)
+    queries_at = lax.broadcasted_iota(jnp.int32, (length, 2 * length), 1) % length
+    allowed = keys_at <= queries_at
+    parts = [(k, v)] if k_low is None else [(k, v), (k_low, v_low)]
+    q_t = (q * jnp.bfloat16(0.125)).T
+    g_t = g.T
+    flipped = [(pk.T, pv.T) for pk, pv in parts]
+    blank = jnp.zeros((64, length), jnp.bfloat16)
+    heads = (slice(0, 64), slice(64, 128))
+    cols = (slice(0, length), slice(length, 2 * length))
+
+    def beside(first, second):
+        return jnp.concatenate(
+            [jnp.concatenate([first, blank], axis=0), jnp.concatenate([blank, second], axis=0)], axis=1
+        )
+
+    def per_head(lefts, rights, extra):
+        found = []
+        if length <= 128:
+            both = 0.0
+            for left, right in zip(lefts, rights):
+                rows = left
+                if extra:
+                    rows = jnp.concatenate([left, jnp.ones((16, left.shape[1]), jnp.bfloat16)], axis=0)
+                both = both + dot(rows, right, NN)
+            for rows, at in zip(heads, cols):
+                found.append((both[rows, at], both[128:129, at] if extra else None))
+            return found
+        for rows, at in zip(heads, cols):
+            one = 0.0
+            for left, right in zip(lefts, rights):
+                mine = left[rows]
+                if extra:
+                    mine = jnp.concatenate([mine, jnp.ones((16, left.shape[1]), jnp.bfloat16)], axis=0)
+                one = one + dot(mine, right[:, at], NN)
+            found.append((one[:64], one[64:65] if extra else None))
+        return found
+
+    q_both, g_both = beside(q_t[:64], q_t[64:]), beside(g_t[:64], g_t[64:])
+    scores = [dot(pk, q_both, NN) for pk, _ in parts]
+    dprobs = [dot(pv, g_both, NN) for _, pv in parts]
+    scores[0] = jnp.where(allowed, scores[0], -1e30)
+    top = functools.reduce(jnp.maximum, [jnp.max(s, axis=0, keepdims=True) for s in scores])
+    weights = [jnp.exp(s - top) for s in scores]
+    low = [w.astype(jnp.bfloat16) for w in weights]
+    summed = per_head([v_t for _, v_t in flipped], low, True)
+    inverse = [1.0 / norm for _, norm in summed]
+    attended = [total * inv for (total, _), inv in zip(summed, inverse)]
+    g_here = [g_t[rows].astype(jnp.float32) for rows in heads]
+    delta = jnp.concatenate(
+        [jnp.sum(a * b, axis=0, keepdims=True) for a, b in zip(g_here, attended)], axis=1
     )
-    zero = jnp.zeros((), jnp.bfloat16)
-    q = q * jnp.bfloat16(0.125)
-    totals = None
-    for head in range(2):
-        mine = (lane < 64) if head == 0 else (lane >= 64)
-        qh, kh, vh, gh = [jnp.where(mine, t, zero) for t in (q, k, v, g)]
-        scores = jnp.where(allowed, dot(qh, k, NT), -1e30)
-        dprobs = dot(gh, v, NT)
-        top = jnp.max(scores, axis=1, keepdims=True)
-        if k_low is not None:
-            scores_low = dot(qh, k_low, NT)
-            dprobs_low = dot(gh, v_low, NT)
-            top = jnp.maximum(top, jnp.max(scores_low, axis=1, keepdims=True))
-        weights = jnp.exp(scores - top)
-        norm = jnp.sum(weights, axis=1, keepdims=True)
-        if k_low is not None:
-            weights_low = jnp.exp(scores_low - top)
-            norm = norm + jnp.sum(weights_low, axis=1, keepdims=True)
-        inverse = 1.0 / norm
-        probs = weights * inverse
-        delta = jnp.sum(probs * dprobs, axis=1, keepdims=True)
-        if k_low is not None:
-            probs_low = weights_low * inverse
-            delta = delta + jnp.sum(probs_low * dprobs_low, axis=1, keepdims=True)
-        ds = (probs * (dprobs - delta)).astype(jnp.bfloat16)
-        pb = probs.astype(jnp.bfloat16)
-        parts = [dot(pb, vh, NN), dot(ds, kh, NN), dot(ds, qh, TN), dot(pb, gh, TN)]
-        if k_low is not None:
-            ds_low = (probs_low * (dprobs_low - delta)).astype(jnp.bfloat16)
-            pb_low = probs_low.astype(jnp.bfloat16)
-            kh_low, vh_low = [jnp.where(mine, t, zero) for t in (k_low, v_low)]
-            parts[0] = parts[0] + dot(pb_low, vh_low, NN)
-            parts[1] = parts[1] + dot(ds_low, kh_low, NN)
-            parts += [dot(ds_low, qh, TN), dot(pb_low, gh, TN)]
-        totals = parts if totals is None else [a + b for a, b in zip(totals, parts)]
-    totals[1] = totals[1] * 0.125
-    return totals
+    ds = [(w * (d - delta)).astype(jnp.bfloat16) for w, d in zip(weights, dprobs)]
+    dq = per_head([k_t for k_t, _ in flipped], ds, False)
+    dq = [total * (inv * 0.125) for (total, _), inv in zip(dq, inverse)]
+    q_scaled = beside(*[(q_t[r].astype(jnp.float32) * inv).astype(jnp.bfloat16) for r, inv in zip(heads, inverse)])
+    g_scaled = beside(*[(gh * inv).astype(jnp.bfloat16) for gh, inv in zip(g_here, inverse)])
+    found = [jnp.concatenate([t.astype(jnp.bfloat16) for t in two], axis=0).T for two in (attended, dq)]
+    for d, w in zip(ds, low):
+        found += [dot(d, q_scaled, NT), dot(w, g_scaled, NT)]
+    return found
 
 
 def body(
@@ -98,15 +121,22 @@
     row_partner = (row, (1 - z_hi) * 4 + y)
     col_partner = ((1 - z_lo) * 8 + xc, col)
 
-    for a in range(4):
-        pltpu.make_async_copy(inputs[a].at[:, :, pl.ds(HALF, HALF)], stage.at[a], st_l.at[a]).start()
+    def stage_copy(a, part, core_of):
+        at = pl.ds(core_of * COL_BLOCK + part * 16, 16)
+        return pltpu.make_async_copy(
+            inputs[a].at[:, at, pl.ds(HALF, HALF)], stage.at[a, :, at], st_l.at[a, part, core_of]
+        )
+
+    for part in range(2):
+        for a in range(4):
+            for core_of in range(2):
+                stage_copy(a, part, core_of).start()
 
     barrier = pltpu.get_barrier_semaphore()
     everyone = [row_peer(d)[1] for d in range(1, 4)] + [col_peer(d)[1] for d in range(1, 8)]
     everyone += [row_partner, col_partner]
     for device in everyone:
         pl.semaphore_signal(barrier, inc=1, device_id=device, device_id_type=MESH)
-    pl.semaphore_wait(barrier, len(everyone))
 
     def lanes(i):
         return pl.ds(pl.multiple_of(i * LANES, LANES), LANES)
@@ -157,51 +187,54 @@
             device_id=col_peer(d)[1], device_id_type=MESH,
         )
 
+    def which(part):
+        return pl.ds(0, 4) if part == 2 else pl.ds(2 * part, 2)
+
     def row_out_copy(i, part, d):
         other, device = row_peer(d)
         return pltpu.make_async_remote_copy(
-            row_out.at[pl.ds(2 * part, 2), pl.ds(i * ROW_STEP, ROW_STEP), pl.ds(other * COLS_HERE, COLS_HERE)],
-            raw_row.at[pl.ds(2 * part, 2), pl.ds(i * ROW_STEP, ROW_STEP), :, lanes(y)],
-            ro_s.at[i, part, d - 1], ro_r.at[i, part, d - 1], device_id=device, device_id_type=MESH,
+            row_out.at[which(part), pl.ds(i * ROW_STEP, ROW_STEP), pl.ds(other * COLS_HERE, COLS_HERE)],
+            raw_row.at[which(part), pl.ds(i * ROW_STEP, ROW_STEP), :, lanes(y)],
+            ro_s.at[i, part % 2, d - 1], ro_r.at[i, part % 2, d - 1], device_id=device, device_id_type=MESH,
         )
 
     def row_out_own(i, part):
         return pltpu.make_async_copy(
-            row_out.at[pl.ds(2 * part, 2), pl.ds(i * ROW_STEP, ROW_STEP), pl.ds(y * COLS_HERE, COLS_HERE)],
-            raw_row.at[pl.ds(2 * part, 2), pl.ds(i * ROW_STEP, ROW_STEP), :, lanes(y)],
-            ro_l.at[i, part],
+            row_out.at[which(part), pl.ds(i * ROW_STEP, ROW_STEP), pl.ds(y * COLS_HERE, COLS_HERE)],
+            raw_row.at[which(part), pl.ds(i * ROW_STEP, ROW_STEP), :, lanes(y)],
+            ro_l.at[i, part % 2],
         )
 
     def row_out_arrival(i, part, d):
         src = (y + 4 - d) % 4
-        place = raw_row.at[pl.ds(2 * part, 2), pl.ds(i * ROW_STEP, ROW_STEP), :, lanes(src)]
-        return pltpu.make_async_remote_copy(
-            place, place, ro_s.at[i, part, d - 1], ro_r.at[i, part, d - 1],
+        place = raw_row.at[which(part), pl.ds(i * ROW_STEP, ROW_STEP), :, lanes(src)]
+        return pltpu.make_async_remote_copy(
+            place, place, ro_s.at[i, part % 2, d - 1], ro_r.at[i, part % 2, d - 1],
             device_id=row_peer(d)[1], device_id_type=MESH,
         )
 
     def col_out_copy(i, part, d):
         other, device = col_peer(d)
         return pltpu.make_async_remote_copy(
-            col_out.at[pl.ds(2 * part, 2), pl.ds(i * COL_STEP, COL_STEP), pl.ds(other * ROWS_HERE, ROWS_HERE)],
-            raw_col.at[pl.ds(2 * part, 2), pl.ds(core * COL_BLOCK + i * COL_STEP, COL_STEP), :, lanes(x)],
-            co_s.at[i, part, d - 1], co_r.at[i, part, d - 1], device_id=device, device_id_type=MESH,
+            col_out.at[which(part), pl.ds(i * COL_STEP, COL_STEP), pl.ds(other * ROWS_HERE, ROWS_HERE)],
+            raw_col.at[which(part), pl.ds(core * COL_BLOCK + i * COL_STEP, COL_STEP), :, lanes(x)],
+            co_s.at[i, part % 2, d - 1], co_r.at[i, part % 2, d - 1], device_id=device, device_id_type=MESH,
         )
 
     def col_out_own(i, part):
         return pltpu.make_async_copy(
-            col_out.at[pl.ds(2 * part, 2), pl.ds(i * COL_STEP, COL_STEP), pl.ds(xc * ROWS_HERE, ROWS_HERE)],
-            raw_col.at[pl.ds(2 * part, 2), pl.ds(core * COL_BLOCK + i * COL_STEP, COL_STEP), :, lanes(x)],
-            co_l.at[i, part],
+            col_out.at[which(part), pl.ds(i * COL_STEP, COL_STEP), pl.ds(xc * ROWS_HERE, ROWS_HERE)],
+            raw_col.at[which(part), pl.ds(core * COL_BLOCK + i * COL_STEP, COL_STEP), :, lanes(x)],
+            co_l.at[i, part % 2],
         )
 
     def col_out_arrival(i, part, d):
         src = (xc + 8 - d) % 8
         place = raw_col.at[
-            pl.ds(2 * part, 2), pl.ds((src % 2) * COL_BLOCK + i * COL_STEP, COL_STEP), :, lanes(src // 2)
+            which(part), pl.ds((src % 2) * COL_BLOCK + i * COL_STEP, COL_STEP), :, lanes(src // 2)
         ]
         return pltpu.make_async_remote_copy(
-            place, place, co_s.at[i, part, d - 1], co_r.at[i, part, d - 1],
+            place, place, co_s.at[i, part % 2, d - 1], co_r.at[i, part % 2, d - 1],
             device_id=col_peer(d)[1], device_id_type=MESH,
         )
 
@@ -222,32 +255,38 @@
             row_in_own(i, a).start()
         return carry
 
-    issue_row(0, 0)
-
     to = lax.broadcasted_iota(jnp.int32, (256, 256), 0)
     frm = lax.broadcasted_iota(jnp.int32, (256, 256), 1)
     turn = jnp.where(frm == (to % 16) * 16 + to // 16, 1.0, 0.0).astype(jnp.bfloat16)
 
     def turn_blocks(part):
-        def one(t, carry):
-            a, at = t // 2, (t % 2) * COL_BLOCK + part * 16
-            block = stage[a, :, pl.ds(pl.multiple_of(at, 16), 16), :].reshape(256, HALF)
-            turned = dot(turn, block, NN).astype(jnp.bfloat16).reshape(16, 16, HALF)
-            send[a, pl.ds(at, 16)] = turned
+        for a in range(4):
+            for core_of in range(2):
+                stage_copy(a, part, core_of).wait()
+
+        def one(a, carry):
+            for core_of in range(2):
+                at = core_of * COL_BLOCK + part * 16
+                block = stage[a, :, pl.ds(at, 16), :].reshape(256, HALF)
+                turned = dot(turn, block, NN).astype(jnp.bfloat16).reshape(16, 16, HALF)
+                send[a, pl.ds(at, 16)] = turned
             return carry
 
-        lax.fori_loop(0, 8, one, 0)
-        for j in range(STEPS // 2):
-            i = part * (STEPS // 2) + j
-            for d in (4, 5, 2, 3, 6, 7, 1):
-                col_in_copy(i, d).start()
-            col_in_own(i).start()
-
-    for a in range(4):
-        pltpu.make_async_copy(inputs[a].at[:, :, pl.ds(HALF, HALF)], stage.at[a], st_l.at[a]).wait()
+        lax.fori_loop(0, 4, one, 0)
+
+    def issue_col(i, carry):
+        for d in (4, 5, 2, 3, 6, 7, 1):
+            col_in_copy(i, d).start()
+        col_in_own(i).start()
+        return carry
+
     turn_blocks(0)
+    pl.semaphore_wait(barrier, len(everyone))
+    issue_row(0, 0)
+    lax.fori_loop(0, STEPS // 2, issue_col, 0)
     lax.fori_loop(1, STEPS // 2, issue_row, 0)
     turn_blocks(1)
+    lax.fori_loop(STEPS // 2, STEPS, issue_col, 0)
     lax.fori_loop(STEPS // 2, STEPS, issue_row, 0)
 
     def send_row(i, part):
@@ -260,8 +299,8 @@
             col_out_copy(i, part, d).start()
         col_out_own(i, part).start()
 
-    def work(upper, box, low, out, part, keep, step, i):
-        def one(n, carry):
+    def work(upper, box, low, out, part, keep, step, unroll, i):
+        def one(n):
             q, k, v, g = [box[a, n] for a in range(4)]
             if upper:
                 found = attend(q, k, v, g, low[0, n], low[1, n])
@@ -275,9 +314,13 @@
                 out[1, n] = found[1].astype(jnp.bfloat16)
                 keep[0, n] = found[2]
                 keep[1, n] = found[3]
+
+        def some(m, carry):
+            for u in range(unroll):
+                one(i * step + m * unroll + u)
             return carry
 
-        lax.fori_loop(i * step, (i + 1) * step, one, 0)
+        lax.fori_loop(0, step // unroll, some, 0)
 
     def finish(half, low, out, keep, step, i):
         half(i, True, low).wait_recv()
@@ -289,8 +332,8 @@
 
         lax.fori_loop(i * step, (i + 1) * step, one, 0)
 
-    def row_step(i):
-        for a in (1, 2, 0, 3):
+    def arrive(i):
+        for a in range(4):
             for d in range(1, 4):
                 row_in_arrival(i, a, d).wait_recv()
             row_in_own(i, a).wait()
@@ -298,18 +341,7 @@
         @pl.when(z_hi == 0)
         def _():
             row_half(i, False, row_in).start()
-            work(False, row_in, row_low, row_out, row_part, row_keep, ROW_STEP, i)
-            send_row(i, 0)
-
-        @pl.when(z_hi == 1)
-        def _():
-            row_half(i, True, row_part).wait_recv()
-            work(True, row_in, row_low, row_out, row_part, row_keep, ROW_STEP, i)
-            row_half(i, True, row_part).start()
-            send_row(i, 0)
-            send_row(i, 1)
-
-    def col_step(i):
+
         for d in range(1, 8):
             col_in_arrival(i, d).wait_recv()
         col_in_own(i).wait()
@@ -317,43 +349,83 @@
         @pl.when(z_lo == 0)
         def _():
             col_half(i, False, col_in).start()
-            work(False, col_in, col_low, col_out, col_part, col_keep, COL_STEP, i)
+
+    def lower_work(i):
+        @pl.when(z_hi == 0)
+        def _():
+            work(False, row_in, row_low, row_out, row_part, row_keep, ROW_STEP, ROW_UNROLL, i)
+            send_row(i, 0)
+
+        @pl.when(z_lo == 0)
+        def _():
+            work(False, col_in, col_low, col_out, col_part, col_keep, COL_STEP, COL_UNROLL, i)
             send_col(i, 0)
 
+    def upper_work(i):
+        @pl.when(z_hi == 1)
+        def _():
+            row_half(i, True, row_part).wait_recv()
+            work(True, row_in, row_low, row_out, row_part, row_keep, ROW_STEP, ROW_UNROLL, i)
+            row_half(i, True, row_part).start()
+            send_row(i, 2)
+
         @pl.when(z_lo == 1)
         def _():
             col_half(i, True, col_part).wait_recv()
-            work(True, col_in, col_low, col_out, col_part, col_keep, COL_STEP, i)
+            work(True, col_in, col_low, col_out, col_part, col_keep, COL_STEP, COL_UNROLL, i)
             col_half(i, True, col_part).start()
-            send_col(i, 0)
-            send_col(i, 1)
-
-    def row_finish(i):
+            send_col(i, 2)
+
+    def finish_lower(i):
         @pl.when(z_hi == 0)
         def _():
             finish(row_half, row_low, row_out, row_keep, ROW_STEP, i)
             send_row(i, 1)
 
-    def col_finish(i):
         @pl.when(z_lo == 0)
         def _():
             finish(col_half, col_low, col_out, col_keep, COL_STEP, i)
             send_col(i, 1)
 
+    arrive(0)
+
     def step(i, carry):
-        row_step(i)
-        col_step(i)
-
-        @pl.when(i > 0)
-        def _():
-            row_finish(i - 1)
-            col_finish(i - 1)
+        @pl.when(i < STEPS - 1)
+        def _():
+            arrive(i + 1)
+
+        lower_work(i)
+        upper_work(i)
+
+        @pl.when(i >= LAG)
+        def _():
+            finish_lower(i - LAG)
 
         return carry
 
     lax.fori_loop(0, STEPS, step, 0)
-    row_finish(STEPS - 1)
-    col_finish(STEPS - 1)
+
+    def late(i, carry):
+        finish_lower(i)
+        return carry
+
+    lax.fori_loop(STEPS - LAG, STEPS, late, 0)
+
+    def drain_out(i, upper, own, copy, arrival, count):
+        @pl.when(upper)
+        def _():
+            own(i, 2).wait()
+            for d in range(1, count):
+                arrival(i, 2, d).wait_recv()
+                copy(i, 2, d).wait_send()
+
+        @pl.when(jnp.logical_not(upper))
+        def _():
+            for part in range(2):
+                own(i, part).wait()
+                for d in range(1, count):
+                    arrival(i, part, d).wait_recv()
+                    copy(i, part, d).wait_send()
 
     def drain(i, carry):
         for a in range(4):
@@ -361,20 +433,10 @@
                 row_in_copy(i, a, d).wait_send()
         for d in range(1, 8):
             col_in_copy(i, d).wait_send()
-        for part in range(2):
-            for d in range(1, 4):
-                row_out_copy(i, part, d).wait_send()
-            for d in range(1, 8):
-                col_out_copy(i, part, d).wait_send()
         row_half(i, True, row_part).wait_send()
         col_half(i, True, col_part).wait_send()
-        for part in range(2):
-            row_out_own(i, part).wait()
-            col_out_own(i, part).wait()
-            for d in range(1, 4):
-                row_out_arrival(i, part, d).wait_recv()
-            for d in range(1, 8):
-                col_out_arrival(i, part, d).wait_recv()
+        drain_out(i, z_hi == 1, row_out_own, row_out_copy, row_out_arrival, 4)
+        drain_out(i, z_lo == 1, col_out_own, col_out_copy, col_out_arrival, 8)
         return carry
 
     lax.fori_loop(0, STEPS, drain, 0)
@@ -409,7 +471,7 @@
         + [dma((STEPS, 2, 3)), dma((STEPS, 2, 3)), dma((STEPS, 2))]
         + [dma((STEPS, 2, 7)), dma((STEPS, 2, 7)), dma((STEPS, 2))]
         + [dma((STEPS,))] * 4
-        + [dma((4,))],
+        + [dma((4, 2, 2))],
         compiler_params=pltpu.CompilerParams(
             collective_id=0, has_side_effects=True, vmem_limit_bytes=60 * 2**20
         ),

time: 169 us -> 135 us (0.80)
  the two profiles are of different devices: /device:TPU:65 before, /device:TPU:1 now
where the time goes in v2:
time: 135 us
  Pallas kernels  132 us (98%)
  local copies, waits for them, and re-layouts  2.18 us (2%)
    pallas_call x1, Pallas kernels, exchange(): pl.pallas_call(body, out_shape=[jax.ShapeDtypeStruct((4, ROWS_HERE, COLS_...  125 us
    pallas_call x1, Pallas kernels, join(): pl.pallas_call(join_body, grid=(COLS_HERE // 16,), out_shape=[shape] * 4,...  6.78 us

profile of v2, /device:TPU:1, one launch (start us, length us, event | category | flops | bytes accessed | tf_op | source)
XLA Modules:
  0.0 135.1 jit_solution(9384266869099420771)
XLA Ops:
  0.6 125.5 %exchange.1 = (bf16[4,16,64,512]{3,2,1,0:T(8,128)(2,1)}, bf16[4,64,16,512]{3,2,1,0:T(8,128)(2,1)}) custom-call(bf16[16,64,1024]{2,1,0:T(8,128)(2,1)} %q_ref.1, bf16[16,64,1024]{2,1,0:T(8,128)(2,1)} %k_ref.1, bf16[16,64,1024]{2,1,0:T(8,128)(2,1)} %v_ref.1, bf16[16,64,1024]{2,1,0:T(8,128)(2,1)} %g_ref.1), custom_call_target="tpu_custom_call" | custom-call | tf_op jit(solution)/shard_map/exchange/pallas_call | solution.py:458
  126.1 0.0 copy-start
  126.1 2.2 %copy-done = bf16[4,16,64,512]{3,2,1,0:T(8,128)(2,1)S(1)} copy-done((bf16[4,16,64,512]{3,2,1,0:T(8,128)(2,1)S(1)}, bf16[4,16,64,512]{3,2,1,0:T(8,128)(2,1)}, u32[]{:S(2)}) %copy-start) | copy-done | bytes 4194328
  128.3 6.8 %join.1 = (bf16[16,64,1024]{2,1,0:T(8,128)(2,1)}, bf16[16,64,1024]{2,1,0:T(8,128)(2,1)}, bf16[16,64,1024]{2,1,0:T(8,128)(2,1)}, bf16[16,64,1024]{2,1,0:T(8,128)(2,1)}) custom-call(bf16[4,16,64,512]{3,2,1,0:T(8,128)(2,1)S(1)} %copy-done, bf16[4,64,16,512]{3,2,1,0:T(8,128)(2,1)} %get-tuple-element.7.col_ref), custom_call_target="tpu_custom_call" | custom-call | tf_op jit(solution)/shard_map/join/pallas_call | solution.py:494
Async XLA Ops:
  126.1 2.2 %copy-start = (bf16[4,16,64,512]{3,2,1,0:T(8,128)(2,1)S(1)}, bf16[4,16,64,512]{3,2,1,0:T(8,128)(2,1)}, u32[]{:S(2)}) copy-start(bf16[4,16,64,512]{3,2,1,0:T(8,128)(2,1)} %get-tuple-element.6.row_ref) | copy-start | bytes 12582916

commit v3 on v2

v3 whole, which is shorter than its diff:
```python
import functools

import jax
import jax.numpy as jnp
from jax import lax
from jax.experimental import pallas as pl
from jax.experimental.pallas import tpu as pltpu
from jax.sharding import PartitionSpec as P

MESH = pl.DeviceIdType.MESH
STEPS = 16
LAG = 5
LANES = 128
HALF = 512
ROWS_HERE = 16
COLS_HERE = 64
ROW_SEQ = 256
COL_SEQ = 128
COL_BLOCK = 32
ROW_STEP = ROWS_HERE // STEPS
COL_STEP = COL_BLOCK // STEPS
ROW_UNROLL = min(ROW_STEP, 2)
COL_UNROLL = min(COL_STEP, 4)
NT = (((1,), (1,)), ((), ()))
NN = (((1,), (0,)), ((), ()))


def dot(a, b, dims):
    return lax.dot_general(a, b, dims, preferred_element_type=jnp.float32)


def beside(first, second):
    blank = jnp.zeros_like(first)
    return jnp.concatenate(
        [jnp.concatenate([first, blank], axis=0), jnp.concatenate([blank, second], axis=0)], axis=1
    )


def per_head(lefts, rights, norms):
    length = rights[0].shape[1] // 2
    heads = (slice(0, 64), slice(64, 128))
    cols = (slice(0, length), slice(length, 2 * length))

    def with_ones(rows):
        if not norms:
            return rows
        return jnp.concatenate([rows, jnp.ones((16, rows.shape[1]), jnp.bfloat16)], axis=0)

    if length <= 128:
        both = sum(dot(with_ones(left), right, NN) for left, right in zip(lefts, rights))
        return [(both[rows, at], both[128:129, at] if norms else None) for rows, at in zip(heads, cols)]
    found = []
    for rows, at in zip(heads, cols):
        one = sum(dot(with_ones(left[rows]), right[:, at], NN) for left, right in zip(lefts, rights))
        found.append((one[:64], one[64:65] if norms else None))
    return found


def over_queries(two):
    return jnp.concatenate(two, axis=1)


def natural(two):
    return jnp.concatenate([t.astype(jnp.bfloat16) for t in two], axis=0).T


def split(pair):
    return pair[:64], pair[64:]


def attend(q, k, v, g, k_low=None, v_low=None):
    length = q.shape[0]
    keys_at = lax.broadcasted_iota(jnp.int32, (length, 2 * length), 0)
    queries_at = lax.broadcasted_iota(jnp.int32, (length, 2 * length), 1) % length
    parts = [(k, v)] if k_low is None else [(k, v), (k_low, v_low)]
    q_t = split((q * jnp.bfloat16(0.125)).T)
    g_t = split(g.T)
    flipped = [(pk.T, pv.T) for pk, pv in parts]
    q_both, g_both = beside(*q_t), beside(*g_t)
    scores = [dot(pk, q_both, NN) for pk, _ in parts]
    dprobs = [dot(pv, g_both, NN) for _, pv in parts]
    scores[0] = jnp.where(keys_at <= queries_at, scores[0], -1e30)
    top = functools.reduce(jnp.maximum, [jnp.max(s, axis=0, keepdims=True) for s in scores])
    weights = [jnp.exp(s - top) for s in scores]
    low = [w.astype(jnp.bfloat16) for w in weights]
    summed = per_head([v_t for _, v_t in flipped], low, True)
    norm = over_queries([n for _, n in summed])
    total = [t for t, _ in summed]
    scale = 1.0 / norm
    inverse = (scale[:, :length], scale[:, length:])
    attended = [t * inv for t, inv in zip(total, inverse)]
    g_here = [one.astype(jnp.float32) for one in g_t]
    delta = over_queries([jnp.sum(a * b, axis=0, keepdims=True) for a, b in zip(g_here, attended)])
    ds = [(w * (d - delta)).astype(jnp.bfloat16) for w, d in zip(weights, dprobs)]
    dq = [t * (inv * 0.125) for (t, _), inv in zip(per_head([k_t for k_t, _ in flipped], ds, False), inverse)]
    q_scaled = beside(*[(t.astype(jnp.float32) * inv).astype(jnp.bfloat16) for t, inv in zip(q_t, inverse)])
    g_scaled = beside(*[(t * inv).astype(jnp.bfloat16) for t, inv in zip(g_here, inverse)])
    found = [natural(attended), natural(dq)]
    for d, w in zip(ds, low):
        found += [dot(d, q_scaled, NT), dot(w, g_scaled, NT)]
    return found


def body(
    q_ref, k_ref, v_ref, g_ref, raw_row, raw_col,
    row_in, row_low, row_out, row_part, row_keep,
    col_in, col_low, col_out, col_part, col_keep,
    stage, send,
    ri_s, ri_r, ci_s, ci_r, ro_s, ro_r, co_s, co_r, rf_s, rf_r, cf_s, cf_r, st_l,
):
    inputs = (k_ref, v_ref, q_ref, g_ref)
    row, col = lax.axis_index("row"), lax.axis_index("col")
    z_lo, xc = row // 8, row % 8
    x, core = xc // 2, xc % 2
    z_hi, y = col // 4, col % 4

    def row_peer(d):
        other = (y + d) % 4
        return other, (row, z_hi * 4 + other)

    def col_peer(d):
        other = (xc + d) % 8
        return other, (z_lo * 8 + other, col)

    row_partner = (row, (1 - z_hi) * 4 + y)
    col_partner = ((1 - z_lo) * 8 + xc, col)

    def stage_copy(a, part, core_of):
        at = pl.ds(core_of * COL_BLOCK + part * 16, 16)
        return pltpu.make_async_copy(
            inputs[a].at[:, at, pl.ds(HALF, HALF)], stage.at[a, :, at], st_l.at[a, part, core_of]
        )

    for part in range(2):
        for a in range(4):
            for core_of in range(2):
                stage_copy(a, part, core_of).start()

    barrier = pltpu.get_barrier_semaphore()
    everyone = [row_peer(d)[1] for d in range(1, 4)] + [col_peer(d)[1] for d in range(1, 8)]
    everyone += [row_partner, col_partner]
    for device in everyone:
        pl.semaphore_signal(barrier, inc=1, device_id=device, device_id_type=MESH)

    def lanes(i):
        return pl.ds(pl.multiple_of(i * LANES, LANES), LANES)

    def row_in_copy(i, a, d):
        other, device = row_peer(d)
        return pltpu.make_async_remote_copy(
            inputs[a].at[pl.ds(i * ROW_STEP, ROW_STEP), :, lanes(other)],
            row_in.at[a, pl.ds(i * ROW_STEP, ROW_STEP), pl.ds(y * COLS_HERE, COLS_HERE)],
            ri_s.at[0], ri_r.at[i, a // 2], device_id=device, device_id_type=MESH,
        )

    def row_in_own(i, a):
        return pltpu.make_async_copy(
            inputs[a].at[pl.ds(i * ROW_STEP, ROW_STEP), :, lanes(y)],
            row_in.at[a, pl.ds(i * ROW_STEP, ROW_STEP), pl.ds(y * COLS_HERE, COLS_HERE)],
            ri_r.at[i, a // 2],
        )

    def col_in_copy(i, pair, d):
        other, device = col_peer(d)
        return pltpu.make_async_remote_copy(
            send.at[pl.ds(2 * pair, 2), pl.ds((other % 2) * COL_BLOCK + i * COL_STEP, COL_STEP), :, lanes(other // 2)],
            col_in.at[pl.ds(2 * pair, 2), pl.ds(i * COL_STEP, COL_STEP), pl.ds(xc * ROWS_HERE, ROWS_HERE)],
            ci_s.at[0], ci_r.at[i, pair], device_id=device, device_id_type=MESH,
        )

    def col_in_own(i, pair):
        return pltpu.make_async_copy(
            send.at[pl.ds(2 * pair, 2), pl.ds(core * COL_BLOCK + i * COL_STEP, COL_STEP), :, lanes(x)],
            col_in.at[pl.ds(2 * pair, 2), pl.ds(i * COL_STEP, COL_STEP), pl.ds(xc * ROWS_HERE, ROWS_HERE)],
            ci_r.at[i, pair],
        )

    def which(part):
        return pl.ds(0, 4) if part == 2 else pl.ds(2 * part, 2)

    def row_out_copy(i, part, d):
        other, device = row_peer(d)
        return pltpu.make_async_remote_copy(
            row_out.at[which(part), pl.ds(i * ROW_STEP, ROW_STEP), pl.ds(other * COLS_HERE, COLS_HERE)],
            raw_row.at[which(part), pl.ds(i * ROW_STEP, ROW_STEP), :, lanes(y)],
            ro_s.at[0], ro_r.at[0], device_id=device, device_id_type=MESH,
        )

    def row_out_own(i, part):
        return pltpu.make_async_copy(
            row_out.at[which(part), pl.ds(i * ROW_STEP, ROW_STEP), pl.ds(y * COLS_HERE, COLS_HERE)],
            raw_row.at[which(part), pl.ds(i * ROW_STEP, ROW_STEP), :, lanes(y)],
            ro_r.at[0],
        )

    def col_out_copy(i, part, d):
        other, device = col_peer(d)
        return pltpu.make_async_remote_copy(
            col_out.at[which(part), pl.ds(i * COL_STEP, COL_STEP), pl.ds(other * ROWS_HERE, ROWS_HERE)],
            raw_col.at[which(part), pl.ds(core * COL_BLOCK + i * COL_STEP, COL_STEP), :, lanes(x)],
            co_s.at[0], co_r.at[0], device_id=device, device_id_type=MESH,
        )

    def col_out_own(i, part):
        return pltpu.make_async_copy(
            col_out.at[which(part), pl.ds(i * COL_STEP, COL_STEP), pl.ds(xc * ROWS_HERE, ROWS_HERE)],
            raw_col.at[which(part), pl.ds(core * COL_BLOCK + i * COL_STEP, COL_STEP), :, lanes(x)],
            co_r.at[0],
        )

    class Side:
        pass

    def make_side(**fields):
        side = Side()
        for name, value in fields.items():
            setattr(side, name, value)
        return side

    def pair_copy(side, i, source):
        return pltpu.make_async_remote_copy(
            source.at[pl.ds(0, 2), pl.ds(i * side.step, side.step)],
            side.low.at[:, pl.ds(i * side.step, side.step)],
            side.f_s.at[0], side.f_r.at[i], device_id=side.partner, device_id_type=MESH,
        )

    def issue_row(i, pair):
        for a in (2 * pair, 2 * pair + 1):
            for d in (2, 1, 3):
                row_in_copy(i, a, d).start()
            row_in_own(i, a).start()

    to = lax.broadcasted_iota(jnp.int32, (256, 256), 0)
    frm = lax.broadcasted_iota(jnp.int32, (256, 256), 1)
    turn = jnp.where(frm == (to % 16) * 16 + to // 16, 1.0, 0.0).astype(jnp.bfloat16)

    def turn_blocks(part, pair):
        for a in (2 * pair, 2 * pair + 1):
            for core_of in range(2):
                stage_copy(a, part, core_of).wait()
                at = core_of * COL_BLOCK + part * 16
                block = stage[a, :, pl.ds(at, 16), :].reshape(256, HALF)
                turned = dot(turn, block, NN).astype(jnp.bfloat16).reshape(16, 16, HALF)
                send[a, pl.ds(at, 16)] = turned

    def issue_col(i, pair):
        for d in (4, 5, 2, 3, 6, 7, 1):
            col_in_copy(i, pair, d).start()
        col_in_own(i, pair).start()

    def issue(i, carry):
        for pair in range(2):
            issue_row(i, pair)
            issue_col(i, pair)
        return carry

    def send_row(i, part):
        for d in (2, 1, 3):
            row_out_copy(i, part, d).start()
        row_out_own(i, part).start()

    def send_col(i, part):
        for d in (4, 5, 2, 3, 6, 7, 1):
            col_out_copy(i, part, d).start()
        col_out_own(i, part).start()

    row_side = make_side(
        upper=z_hi == 1, step=ROW_STEP, unroll=ROW_UNROLL, length=ROW_SEQ, partner=row_partner,
        box=row_in, low=row_low, out=row_out, part=row_part, keep=row_keep, f_s=rf_s, f_r=rf_r,
        send=send_row,
    )
    col_side = make_side(
        upper=z_lo == 1, step=COL_STEP, unroll=COL_UNROLL, length=COL_SEQ, partner=col_partner,
        box=col_in, low=col_low, out=col_out, part=col_part, keep=col_keep, f_s=cf_s, f_r=cf_r,
        send=send_col,
    )

    def each(side, i, one):
        def some(m, carry):
            for u in range(side.unroll):
                one(i * side.step + m * side.unroll + u)
            return carry

        lax.fori_loop(0, side.step // side.unroll, some, 0)

    def bf16(value):
        return value.astype(jnp.bfloat16)

    def begin(side, i):
        def lower_one(n):
            k, v, q, g = [side.box[a, n] for a in range(4)]
            found = attend(q, k, v, g)
            side.out[0, n] = found[0]
            side.out[1, n] = found[1]
            side.keep[0, n] = found[2]
            side.keep[1, n] = found[3]

        def upper_one(n):
            k, v, q, g = [side.box[a, n] for a in range(4)]
            found = attend(q, k, v, g, side.low[0, n], side.low[1, n])
            for a in range(4):
                side.out[a, n] = bf16(found[a])
            side.part[0, n] = bf16(found[4])
            side.part[1, n] = bf16(found[5])

        @pl.when(jnp.logical_not(side.upper))
        def _():
            each(side, i, lower_one)
            side.send(i, 0)

        @pl.when(side.upper)
        def _():
            pair_copy(side, i, side.part).wait_recv()
            each(side, i, upper_one)
            pair_copy(side, i, side.part).start()
            side.send(i, 2)

    def finish(side, i):
        def one(n):
            for a in range(2):
                side.out[2 + a, n] = bf16(side.keep[a, n] + side.low[a, n].astype(jnp.float32))

        @pl.when(jnp.logical_not(side.upper))
        def _():
            pair_copy(side, i, side.part).wait_recv()
            each(side, i, one)
            side.send(i, 1)

    def whole(ref, semaphore):
        pltpu.make_async_copy(ref, ref, semaphore).wait()

    def arrive_row(i, pair):
        whole(row_in.at[pl.ds(2 * pair, 2), pl.ds(i * ROW_STEP, ROW_STEP)], ri_r.at[i, pair])

    def arrive_col(i, pair):
        whole(col_in.at[pl.ds(2 * pair, 2), pl.ds(i * COL_STEP, COL_STEP)], ci_r.at[i, pair])

    def arrive(i):
        arrive_row(i, 0)

        @pl.when(z_hi == 0)
        def _():
            pair_copy(row_side, i, row_in).start()

        arrive_col(i, 0)

        @pl.when(z_lo == 0)
        def _():
            pair_copy(col_side, i, col_in).start()

        arrive_row(i, 1)
        arrive_col(i, 1)

    turn_blocks(0, 0)
    pl.semaphore_wait(barrier, len(everyone))
    issue_row(0, 0)
    issue_col(0, 0)
    issue_row(0, 1)
    turn_blocks(0, 1)
    issue_col(0, 1)
    issue(1, 0)
    arrive(0)
    lax.fori_loop(2, STEPS // 2, issue, 0)
    turn_blocks(1, 0)
    turn_blocks(1, 1)
    lax.fori_loop(STEPS // 2, STEPS, issue, 0)

    def step(i, carry):
        @pl.when(i < STEPS - 1)
        def _():
            arrive(i + 1)

        @pl.when(i < STEPS)
        def _():
            for side in (row_side, col_side):
                begin(side, i)

        @pl.when(i >= LAG)
        def _():
            for side in (row_side, col_side):
                finish(side, i - LAG)

        return carry

    lax.fori_loop(0, STEPS + LAG, step, 0)

    whole(row_in.at[pl.ds(0, 3)], ri_s.at[0])
    whole(col_in.at[:, pl.ds(0, COL_BLOCK * 7 // 8)], ci_s.at[0])
    for side in (row_side, col_side):
        whole(side.low, side.f_s.at[0])

    whole(row_out.at[pl.ds(0, 3)], ro_s.at[0])
    whole(col_out.at[:, pl.ds(0, COL_BLOCK * 7 // 8)], co_s.at[0])
    whole(raw_row, ro_r.at[0])
    whole(raw_col, co_r.at[0])


def exchange(queries, keys, values, grad_output):
    bf16, f32 = jnp.bfloat16, jnp.float32
    dma = pltpu.SemaphoreType.DMA

    def side(many, length):
        return [
            pltpu.VMEM((4, many, length, LANES), bf16),
            pltpu.VMEM((2, many, length, LANES), bf16),
            pltpu.VMEM((4, many, length, LANES), bf16),
            pltpu.VMEM((2, many, length, LANES), bf16),
            pltpu.VMEM((2, many, length, LANES), f32),
        ]

    return pl.pallas_call(
        body,
        out_shape=[
            jax.ShapeDtypeStruct((4, ROWS_HERE, COLS_HERE, HALF), bf16),
            jax.ShapeDtypeStruct((4, COLS_HERE, ROWS_HERE, HALF), bf16),
        ],
        in_specs=[pl.BlockSpec(memory_space=pl.ANY)] * 4,
        out_specs=[pl.BlockSpec(memory_space=pl.ANY)] * 2,
        scratch_shapes=side(ROWS_HERE, ROW_SEQ)
        + side(COL_BLOCK, COL_SEQ)
        + [pltpu.VMEM((4, ROWS_HERE, COLS_HERE, HALF), bf16), pltpu.VMEM((4, COLS_HERE, ROWS_HERE, HALF), bf16)]
        + [dma((1,)), dma((STEPS, 2)), dma((1,)), dma((STEPS, 2))]
        + [dma((1,))] * 4
        + [dma((1,)), dma((STEPS,))] * 2
        + [dma((4, 2, 2))],
        compiler_params=pltpu.CompilerParams(
            collective_id=0, has_side_effects=True, vmem_limit_bytes=60 * 2**20
        ),
        name="exchange",
    )(queries, keys, values, grad_output)


def join_body(row_ref, col_ref, *outs):
    part = pl.program_id(1)

    @pl.when(part == 0)
    def _():
        for a in range(4):
            outs[a][...] = row_ref[a]

    @pl.when(part == 1)
    def _():
        to = lax.broadcasted_iota(jnp.int32, (256, 256), 0)
        frm = lax.broadcasted_iota(jnp.int32, (256, 256), 1)
        turn = jnp.where(frm == (to % 16) * 16 + to // 16, 1.0, 0.0).astype(jnp.bfloat16)
        for a in range(4):
            turned = dot(turn, col_ref[a].reshape(256, HALF), NN)
            outs[a][...] = turned.astype(jnp.bfloat16).reshape(16, 16, HALF)


def join(raw_row, raw_col):
    shape = jax.ShapeDtypeStruct((ROWS_HERE, COLS_HERE, 2 * HALF), jnp.bfloat16)
    return pl.pallas_call(
        join_body,
        grid=(COLS_HERE // 16, 2),
        out_shape=[shape] * 4,
        in_specs=[
            pl.BlockSpec((4, ROWS_HERE, 16, HALF), lambda i, j: (0, 0, i, 0)),
            pl.BlockSpec((4, 16, ROWS_HERE, HALF), lambda i, j: (0, i, 0, 0)),
        ],
        out_specs=[pl.BlockSpec((ROWS_HERE, 16, HALF), lambda i, j: (0, i, j))] * 4,
        compiler_params=pltpu.CompilerParams(vmem_limit_bytes=62 * 2**20),
        name="join",
    )(raw_row, raw_col)


def on_device(queries, keys, values, grad_output):
    raw_row, raw_col = exchange(queries, keys, values, grad_output)
    return tuple(join(raw_row, raw_col))


def solution(mesh):
    spec = P("row", "col", None)
    return jax.shard_map(
        on_device, mesh=mesh, in_specs=(spec,) * 4, out_specs=(spec,) * 4, check_vma=False
    )
```

time: 135 us -> 128 us (0.948)
  the two profiles are of different devices: /device:TPU:1 before, /device:TPU:32 now
where the time goes in v3:
time: 128 us; the launch traced here: 127 us
  Pallas kernels  127 us (99%)
    pallas_call x1, Pallas kernels, exchange(): pl.pallas_call(body, out_shape=[jax.ShapeDtypeStruct((4, ROWS_HERE, COLS_...  116 us
    pallas_call x1, Pallas kernels, join(): pl.pallas_call(join_body, grid=(COLS_HERE // 16, 2), out_shape=[shape] *...  10.3 us

profile of v3, /device:TPU:32, one launch (start us, length us, event | category | flops | bytes accessed | tf_op | source)
XLA Modules:
  0.0 127.3 jit_solution(12505444441033530363)
XLA Ops:
  0.6 116.4 %exchange.1 = (bf16[4,16,64,512]{3,2,1,0:T(8,128)(2,1)}, bf16[4,64,16,512]{3,2,1,0:T(8,128)(2,1)}) custom-call(bf16[16,64,1024]{2,1,0:T(8,128)(2,1)} %q_ref.1, bf16[16,64,1024]{2,1,0:T(8,128)(2,1)} %k_ref.1, bf16[16,64,1024]{2,1,0:T(8,128)(2,1)} %v_ref.1, bf16[16,64,1024]{2,1,0:T(8,128)(2,1)} %g_ref.1), custom_call_target="tpu_custom_call" | custom-call | tf_op jit(solution)/shard_map/exchange/pallas_call | solution.py:411
  117.0 10.3 %join.1 = (bf16[16,64,1024]{2,1,0:T(8,128)(2,1)}, bf16[16,64,1024]{2,1,0:T(8,128)(2,1)}, bf16[16,64,1024]{2,1,0:T(8,128)(2,1)}, bf16[16,64,1024]{2,1,0:T(8,128)(2,1)}) custom-call(bf16[4,16,64,512]{3,2,1,0:T(8,128)(2,1)} %get-tuple-element.6.row_ref, bf16[4,64,16,512]{3,2,1,0:T(8,128)(2,1)} %get-tuple-element.7.col_ref), custom_call_target="tpu_custom_call" | custom-call | tf_op jit(solution)/shard_map/join/pallas_call | solution.py:453

commit v4 on v3

--- a/solution.py
+++ b/solution.py
@@ -9,7 +9,7 @@
 
 MESH = pl.DeviceIdType.MESH
 STEPS = 16
-LAG = 5
+LAG = 1
 LANES = 128
 HALF = 512
 ROWS_HERE = 16
@@ -230,18 +230,12 @@
                 row_in_copy(i, a, d).start()
             row_in_own(i, a).start()
 
-    to = lax.broadcasted_iota(jnp.int32, (256, 256), 0)
-    frm = lax.broadcasted_iota(jnp.int32, (256, 256), 1)
-    turn = jnp.where(frm == (to % 16) * 16 + to // 16, 1.0, 0.0).astype(jnp.bfloat16)
-
     def turn_blocks(part, pair):
         for a in (2 * pair, 2 * pair + 1):
             for core_of in range(2):
                 stage_copy(a, part, core_of).wait()
                 at = core_of * COL_BLOCK + part * 16
-                block = stage[a, :, pl.ds(at, 16), :].reshape(256, HALF)
-                turned = dot(turn, block, NN).astype(jnp.bfloat16).reshape(16, 16, HALF)
-                send[a, pl.ds(at, 16)] = turned
+                send[a, pl.ds(at, 16)] = jnp.swapaxes(stage[a, :, pl.ds(at, 16), :], 0, 1)
 
     def issue_col(i, pair):
         for d in (4, 5, 2, 3, 6, 7, 1):
@@ -286,7 +280,7 @@
     def bf16(value):
         return value.astype(jnp.bfloat16)
 
-    def begin(side, i):
+    def begin(side, i, upper):
         def lower_one(n):
             k, v, q, g = [side.box[a, n] for a in range(4)]
             found = attend(q, k, v, g)
@@ -303,13 +297,12 @@
             side.part[0, n] = bf16(found[4])
             side.part[1, n] = bf16(found[5])
 
-        @pl.when(jnp.logical_not(side.upper))
-        def _():
-            each(side, i, lower_one)
-            side.send(i, 0)
-
-        @pl.when(side.upper)
-        def _():
+        @pl.when(jnp.logical_not(side.upper) if not upper else side.upper)
+        def _():
+            if not upper:
+                each(side, i, lower_one)
+                side.send(i, 0)
+                return
             pair_copy(side, i, side.part).wait_recv()
             each(side, i, upper_one)
             pair_copy(side, i, side.part).start()
@@ -335,7 +328,7 @@
     def arrive_col(i, pair):
         whole(col_in.at[pl.ds(2 * pair, 2), pl.ds(i * COL_STEP, COL_STEP)], ci_r.at[i, pair])
 
-    def arrive(i):
+    def arrive(i, carry):
         arrive_row(i, 0)
 
         @pl.when(z_hi == 0)
@@ -350,6 +343,7 @@
 
         arrive_row(i, 1)
         arrive_col(i, 1)
+        return carry
 
     turn_blocks(0, 0)
     pl.semaphore_wait(barrier, len(everyone))
@@ -359,21 +353,25 @@
     turn_blocks(0, 1)
     issue_col(0, 1)
     issue(1, 0)
-    arrive(0)
+    arrive(0, 0)
     lax.fori_loop(2, STEPS // 2, issue, 0)
     turn_blocks(1, 0)
     turn_blocks(1, 1)
     lax.fori_loop(STEPS // 2, STEPS, issue, 0)
 
+    both_upper = jnp.logical_and(z_hi == 1, z_lo == 1)
+
+    def until(i):
+        return jnp.minimum(jnp.where(both_upper, i + 2, 2 * i + 3), STEPS)
+
     def step(i, carry):
-        @pl.when(i < STEPS - 1)
-        def _():
-            arrive(i + 1)
+        lax.fori_loop(jnp.where(both_upper, i + 1, 2 * i + 1), until(i), arrive, 0)
 
         @pl.when(i < STEPS)
         def _():
-            for side in (row_side, col_side):
-                begin(side, i)
+            for upper in (False, True):
+                for side in (row_side, col_side):
+                    begin(side, i, upper)
 
         @pl.when(i >= LAG)
         def _():
@@ -430,35 +428,56 @@
     )(queries, keys, values, grad_output)
 
 
-def join_body(row_ref, col_ref, *outs):
-    part = pl.program_id(1)
-
-    @pl.when(part == 0)
-    def _():
-        for a in range(4):
-            outs[a][...] = row_ref[a]
-
-    @pl.when(part == 1)
-    def _():
-        to = lax.broadcasted_iota(jnp.int32, (256, 256), 0)
-        frm = lax.broadcasted_iota(jnp.int32, (256, 256), 1)
-        turn = jnp.where(frm == (to % 16) * 16 + to // 16, 1.0, 0.0).astype(jnp.bfloat16)
-        for a in range(4):
-            turned = dot(turn, col_ref[a].reshape(256, HALF), NN)
-            outs[a][...] = turned.astype(jnp.bfloat16).reshape(16, 16, HALF)
+def join_body(row_ref, col_ref, out_0, out_1, out_2, out_3, rows, cols, turned, row_in, row_out, col_in, col_out):
+    outs = (out_0, out_1, out_2, out_3)
+    blocks = COLS_HERE // 16
+
+    def load_row(a):
+        return pltpu.make_async_copy(row_ref.at[a], rows.at[a], row_in.at[a])
+
+    def store_row(a):
+        return pltpu.make_async_copy(rows.at[a], outs[a].at[:, :, pl.ds(0, HALF)], row_out.at[a])
+
+    def load_col(a, b):
+        at = pl.ds(b * 16, 16)
+        return pltpu.make_async_copy(col_ref.at[a, at], cols.at[a, at], col_in.at[a, b])
+
+    def store_col(a, b):
+        at = pl.ds(b * 16, 16)
+        return pltpu.make_async_copy(turned.at[a, :, at], outs[a].at[:, at, pl.ds(HALF, HALF)], col_out.at[a, b])
+
+    for a in range(4):
+        for b in range(blocks):
+            load_col(a, b).start()
+        load_row(a).start()
+    for a in range(4):
+        for b in range(blocks):
+            load_col(a, b).wait()
+            at = pl.ds(b * 16, 16)
+            turned[a, :, at] = jnp.swapaxes(cols[a, at], 0, 1)
+            store_col(a, b).start()
+        load_row(a).wait()
+        store_row(a).start()
+    for a in range(4):
+        for b in range(blocks):
+            store_col(a, b).wait()
+        store_row(a).wait()
 
 
 def join(raw_row, raw_col):
     shape = jax.ShapeDtypeStruct((ROWS_HERE, COLS_HERE, 2 * HALF), jnp.bfloat16)
+    dma = pltpu.SemaphoreType.DMA
     return pl.pallas_call(
         join_body,
-        grid=(COLS_HERE // 16, 2),
         out_shape=[shape] * 4,
-        in_specs=[
-            pl.BlockSpec((4, ROWS_HERE, 16, HALF), lambda i, j: (0, 0, i, 0)),
-            pl.BlockSpec((4, 16, ROWS_HERE, HALF), lambda i, j: (0, i, 0, 0)),
+        in_specs=[pl.BlockSpec(memory_space=pl.ANY)] * 2,
+        out_specs=[pl.BlockSpec(memory_space=pl.ANY)] * 4,
+        scratch_shapes=[
+            pltpu.VMEM((4, ROWS_HERE, COLS_HERE, HALF), jnp.bfloat16),
+            pltpu.VMEM((4, COLS_HERE, ROWS_HERE, HALF), jnp.bfloat16),
+            pltpu.VMEM((4, ROWS_HERE, COLS_HERE, HALF), jnp.bfloat16),
+            dma((4,)), dma((4,)), dma((4, COLS_HERE // 16)), dma((4, COLS_HERE // 16)),
         ],
-        out_specs=[pl.BlockSpec((ROWS_HERE, 16, HALF), lambda i, j: (0, i, j))] * 4,
         compiler_params=pltpu.CompilerParams(vmem_limit_bytes=62 * 2**20),
         name="join",
     )(raw_row, raw_col)

time: 128 us -> 120 us (0.938)
  the two profiles are of different devices: /device:TPU:32 before, /device:TPU:1 now
where the time goes in v4:
time: 120 us
  Pallas kernels  119 us (99%)
    pallas_call x1, Pallas kernels, exchange(): pl.pallas_call(body, out_shape=[jax.ShapeDtypeStruct((4, ROWS_HERE, COLS_...  113 us
    pallas_call x1, Pallas kernels, join(): pl.pallas_call(join_body, out_shape=[shape] * 4, in_specs=[pl.BlockSpec(m...  5.89 us

profile of v4, /device:TPU:1, one launch (start us, length us, event | category | flops | bytes accessed | tf_op | source)
XLA Modules:
  0.0 119.6 jit_solution(15627332783523639401)
XLA Ops:
  0.6 113.1 %exchange.1 = (bf16[4,16,64,512]{3,2,1,0:T(8,128)(2,1)}, bf16[4,64,16,512]{3,2,1,0:T(8,128)(2,1)}) custom-call(bf16[16,64,1024]{2,1,0:T(8,128)(2,1)} %q_ref.1, bf16[16,64,1024]{2,1,0:T(8,128)(2,1)} %k_ref.1, bf16[16,64,1024]{2,1,0:T(8,128)(2,1)} %v_ref.1, bf16[16,64,1024]{2,1,0:T(8,128)(2,1)} %g_ref.1), custom_call_target="tpu_custom_call" | custom-call | tf_op jit(solution)/shard_map/exchange/pallas_call | solution.py:409
  113.7 5.9 %join.1 = (bf16[16,64,1024]{2,1,0:T(8,128)(2,1)}, bf16[16,64,1024]{2,1,0:T(8,128)(2,1)}, bf16[16,64,1024]{2,1,0:T(8,128)(2,1)}, bf16[16,64,1024]{2,1,0:T(8,128)(2,1)}) custom-call(bf16[4,16,64,512]{3,2,1,0:T(8,128)(2,1)} %get-tuple-element.6.row_ref, bf16[4,64,16,512]{3,2,1,0:T(8,128)(2,1)} %get-tuple-element.7.col_ref), custom_call_target="tpu_custom_call" | custom-call | tf_op jit(solution)/shard_map/join/pallas_call | solution.py:470

commit v5 on v4

--- a/solution.py
+++ b/solution.py
@@ -9,7 +9,8 @@
 
 MESH = pl.DeviceIdType.MESH
 STEPS = 16
-LAG = 1
+AHEAD = 4
+LAG, LONG_LAG = 1, 5
 LANES = 128
 HALF = 512
 ROWS_HERE = 16
@@ -131,10 +132,6 @@
             inputs[a].at[:, at, pl.ds(HALF, HALF)], stage.at[a, :, at], st_l.at[a, part, core_of]
         )
 
-    for part in range(2):
-        for a in range(4):
-            for core_of in range(2):
-                stage_copy(a, part, core_of).start()
 
     barrier = pltpu.get_barrier_semaphore()
     everyone = [row_peer(d)[1] for d in range(1, 4)] + [col_peer(d)[1] for d in range(1, 8)]
@@ -222,6 +219,21 @@
             source.at[pl.ds(0, 2), pl.ds(i * side.step, side.step)],
             side.low.at[:, pl.ds(i * side.step, side.step)],
             side.f_s.at[0], side.f_r.at[i], device_id=side.partner, device_id_type=MESH,
+        )
+
+    def ahead_copy(i, a):
+        return pltpu.make_async_remote_copy(
+            inputs[a].at[pl.ds(i * ROW_STEP, ROW_STEP), :, lanes(y)],
+            row_low.at[a, pl.ds(i * ROW_STEP, ROW_STEP), pl.ds(y * COLS_HERE, COLS_HERE)],
+            rf_s.at[0], rf_r.at[i], device_id=row_partner, device_id_type=MESH,
+        )
+
+    def rest_copy(i, d):
+        columns = pl.ds((y + d) % 4 * COLS_HERE, COLS_HERE)
+        return pltpu.make_async_remote_copy(
+            row_in.at[pl.ds(0, 2), pl.ds(i * ROW_STEP, ROW_STEP), columns],
+            row_low.at[:, pl.ds(i * ROW_STEP, ROW_STEP), columns],
+            rf_s.at[0], rf_r.at[i], device_id=row_partner, device_id_type=MESH,
         )
 
     def issue_row(i, pair):
@@ -333,7 +345,14 @@
 
         @pl.when(z_hi == 0)
         def _():
-            pair_copy(row_side, i, row_in).start()
+            @pl.when(i < AHEAD)
+            def _():
+                for d in range(1, 4):
+                    rest_copy(i, d).start()
+
+            @pl.when(i >= AHEAD)
+            def _():
+                pair_copy(row_side, i, row_in).start()
 
         arrive_col(i, 0)
 
@@ -345,27 +364,45 @@
         arrive_col(i, 1)
         return carry
 
+    def stage_part(part):
+        for a in range(4):
+            for core_of in range(2):
+                stage_copy(a, part, core_of).start()
+
+    stage_part(0)
     turn_blocks(0, 0)
     pl.semaphore_wait(barrier, len(everyone))
     issue_row(0, 0)
+
+    @pl.when(z_hi == 0)
+    def _():
+        for i in range(AHEAD):
+            for a in range(2):
+                ahead_copy(i, a).start()
+
     issue_col(0, 0)
     issue_row(0, 1)
     turn_blocks(0, 1)
     issue_col(0, 1)
     issue(1, 0)
+    stage_part(1)
     arrive(0, 0)
-    lax.fori_loop(2, STEPS // 2, issue, 0)
-    turn_blocks(1, 0)
-    turn_blocks(1, 1)
-    lax.fori_loop(STEPS // 2, STEPS, issue, 0)
+    lax.fori_loop(2, 4, issue, 0)
 
     both_upper = jnp.logical_and(z_hi == 1, z_lo == 1)
+    lag = jnp.where(z_hi + z_lo == 0, LONG_LAG, LAG)
 
     def until(i):
-        return jnp.minimum(jnp.where(both_upper, i + 2, 2 * i + 3), STEPS)
+        return jnp.minimum(jnp.where(both_upper, i + 1, 2 * i + 3), STEPS)
 
     def step(i, carry):
-        lax.fori_loop(jnp.where(both_upper, i + 1, 2 * i + 1), until(i), arrive, 0)
+        @pl.when(i == STEPS // 4 - 2)
+        def _():
+            turn_blocks(1, 0)
+            turn_blocks(1, 1)
+
+        lax.fori_loop(2 * i + 4, jnp.minimum(2 * i + 6, STEPS), issue, 0)
+        lax.fori_loop(jnp.where(both_upper, jnp.maximum(i, 1), 2 * i + 1), until(i), arrive, 0)
 
         @pl.when(i < STEPS)
         def _():
@@ -373,14 +410,14 @@
                 for side in (row_side, col_side):
                     begin(side, i, upper)
 
-        @pl.when(i >= LAG)
+        @pl.when(jnp.logical_and(i >= lag, i < STEPS + lag))
         def _():
             for side in (row_side, col_side):
-                finish(side, i - LAG)
+                finish(side, i - lag)
 
         return carry
 
-    lax.fori_loop(0, STEPS + LAG, step, 0)
+    lax.fori_loop(0, STEPS + LONG_LAG, step, 0)
 
     whole(row_in.at[pl.ds(0, 3)], ri_s.at[0])
     whole(col_in.at[:, pl.ds(0, COL_BLOCK * 7 // 8)], ci_s.at[0])

time: 120 us -> 119 us (level)
  no operation moved by 1% of the time
where the time goes in v5:
time: 119 us
  Pallas kernels  119 us (100%)
    pallas_call x1, Pallas kernels, exchange(): pl.pallas_call(body, out_shape=[jax.ShapeDtypeStruct((4, ROWS_HERE, COLS_...  113 us
    pallas_call x1, Pallas kernels, join(): pl.pallas_call(join_body, out_shape=[shape] * 4, in_specs=[pl.BlockSpec(m...  5.89 us

profile of v5, /device:TPU:1, one launch (start us, length us, event | category | flops | bytes accessed | tf_op | source)
XLA Modules:
  0.0 119.4 jit_solution(18006753601766495045)
XLA Ops:
  0.6 112.8 %exchange.1 = (bf16[4,16,64,512]{3,2,1,0:T(8,128)(2,1)}, bf16[4,64,16,512]{3,2,1,0:T(8,128)(2,1)}) custom-call(bf16[16,64,1024]{2,1,0:T(8,128)(2,1)} %q_ref.1, bf16[16,64,1024]{2,1,0:T(8,128)(2,1)} %k_ref.1, bf16[16,64,1024]{2,1,0:T(8,128)(2,1)} %v_ref.1, bf16[16,64,1024]{2,1,0:T(8,128)(2,1)} %g_ref.1), custom_call_target="tpu_custom_call" | custom-call | tf_op jit(solution)/shard_map/exchange/pallas_call | solution.py:446
  113.5 5.9 %join.1 = (bf16[16,64,1024]{2,1,0:T(8,128)(2,1)}, bf16[16,64,1024]{2,1,0:T(8,128)(2,1)}, bf16[16,64,1024]{2,1,0:T(8,128)(2,1)}, bf16[16,64,1024]{2,1,0:T(8,128)(2,1)}) custom-call(bf16[4,16,64,512]{3,2,1,0:T(8,128)(2,1)} %get-tuple-element.6.row_ref, bf16[4,64,16,512]{3,2,1,0:T(8,128)(2,1)} %get-tuple-element.7.col_ref), custom_call_target="tpu_custom_call" | custom-call | tf_op jit(solution)/shard_map/join/pallas_call | solution.py:507

commit v6 on v5

--- a/solution.py
+++ b/solution.py
@@ -9,7 +9,7 @@
 
 MESH = pl.DeviceIdType.MESH
 STEPS = 16
-AHEAD = 4
+AHEAD, FAR_AHEAD = 4, 8
 LAG, LONG_LAG = 1, 5
 LANES = 128
 HALF = 512
@@ -345,12 +345,12 @@
 
         @pl.when(z_hi == 0)
         def _():
-            @pl.when(i < AHEAD)
+            @pl.when(i < ahead)
             def _():
                 for d in range(1, 4):
                     rest_copy(i, d).start()
 
-            @pl.when(i >= AHEAD)
+            @pl.when(i >= ahead)
             def _():
                 pair_copy(row_side, i, row_in).start()
 
@@ -374,11 +374,16 @@
     pl.semaphore_wait(barrier, len(everyone))
     issue_row(0, 0)
 
+    def send_ahead(i, carry):
+        for a in range(2):
+            ahead_copy(i, a).start()
+        return carry
+
+    ahead = jnp.where(z_lo == 0, FAR_AHEAD, AHEAD)
+
     @pl.when(z_hi == 0)
     def _():
-        for i in range(AHEAD):
-            for a in range(2):
-                ahead_copy(i, a).start()
+        lax.fori_loop(0, ahead, send_ahead, 0)
 
     issue_col(0, 0)
     issue_row(0, 1)

time: 119 us -> 120 us (level)
  no operation moved by 1% of the time
where the time goes in v6:
time: 120 us; the launch traced here: 119 us
  Pallas kernels  119 us (99%)
    pallas_call x1, Pallas kernels, exchange(): pl.pallas_call(body, out_shape=[jax.ShapeDtypeStruct((4, ROWS_HERE, COLS_...  113 us
    pallas_call x1, Pallas kernels, join(): pl.pallas_call(join_body, out_shape=[shape] * 4, in_specs=[pl.BlockSpec(m...  5.89 us

profile of v6, /device:TPU:1, one launch (start us, length us, event | category | flops | bytes accessed | tf_op | source)
XLA Modules:
  0.0 119.4 jit_solution(12746985366503063980)
XLA Ops:
  0.6 112.8 %exchange.1 = (bf16[4,16,64,512]{3,2,1,0:T(8,128)(2,1)}, bf16[4,64,16,512]{3,2,1,0:T(8,128)(2,1)}) custom-call(bf16[16,64,1024]{2,1,0:T(8,128)(2,1)} %q_ref.1, bf16[16,64,1024]{2,1,0:T(8,128)(2,1)} %k_ref.1, bf16[16,64,1024]{2,1,0:T(8,128)(2,1)} %v_ref.1, bf16[16,64,1024]{2,1,0:T(8,128)(2,1)} %g_ref.1), custom_call_target="tpu_custom_call" | custom-call | tf_op jit(solution)/shard_map/exchange/pallas_call | solution.py:451
  113.5 5.9 %join.1 = (bf16[16,64,1024]{2,1,0:T(8,128)(2,1)}, bf16[16,64,1024]{2,1,0:T(8,128)(2,1)}, bf16[16,64,1024]{2,1,0:T(8,128)(2,1)}, bf16[16,64,1024]{2,1,0:T(8,128)(2,1)}) custom-call(bf16[4,16,64,512]{3,2,1,0:T(8,128)(2,1)} %get-tuple-element.6.row_ref, bf16[4,64,16,512]{3,2,1,0:T(8,128)(2,1)} %get-tuple-element.7.col_ref), custom_call_target="tpu_custom_call" | custom-call | tf_op jit(solution)/shard_map/join/pallas_call | solution.py:512
